TPU v7x, 256 devices: a whole 4x4x8 slice. The times are simulated.
256 devices in a mesh: dp: 8 (over x, core), fsdp: 32 (over y, z).
Axes of the slice: x: 4, y: 4, z: 8, core: 2. Of those that a mesh axis runs over, the one named last changes fastest.
Arguments:
- gradients: bfloat16 [8, 512, 65536], P('dp', 'fsdp'), may hold values from -36 to 36
Outputs:
- update: bfloat16 [512, 32, 8, 256], P('fsdp', None, 'dp')
All inputs are finite; a program needn't handle non-finite values.
Results may differ from a plain program's by a relative error of at most 0.0077.
Values may be sent and summed in bfloat16 or wider, within the bound.
No kernel may reach another device: no remote copies, remote signals or barrier semaphores. Data moves between devices by JAX's collectives and lax.ppermute only.
A program may use at most 64 MiB of HBM per device.

v0:
```python
import jax
import jax.numpy as jnp
from jax import lax
from jax.sharding import PartitionSpec as P

ITERS = 6


def partner_2(x, axis, apart):
    return lax.ppermute(x, axis, [(i, i ^ 1 << apart) for i in range(lax.axis_size(axis))])


def inverse_root(statistic):
    identity = jnp.eye(statistic.shape[0], dtype=jnp.float32)
    trace_sum = jnp.trace(statistic)
    moment = statistic / trace_sum
    inverse = identity * trace_sum ** (-0.25)
    for iteration in range(ITERS):
        factor = (5.0 * identity - moment) * 0.25
        inverse = jnp.dot(
            inverse, factor, precision=lax.Precision.HIGHEST, preferred_element_type=jnp.float32
        )
        if iteration + 1 < ITERS:
            square = jnp.dot(
                factor, factor, precision=lax.Precision.HIGHEST, preferred_element_type=jnp.float32
            )
            fourth = jnp.dot(
                square, square, precision=lax.Precision.HIGHEST, preferred_element_type=jnp.float32
            )
            moment = jnp.dot(
                fourth, moment, precision=lax.Precision.HIGHEST, preferred_element_type=jnp.float32
            )
    return inverse


def orient_blocks(blocks, side_bit):
    return jnp.where(side_bit == 0, jnp.swapaxes(blocks, 1, 2), blocks)


def per_device(gradients):
    groups = lax.axis_size("dp")
    owners = lax.axis_size("fsdp")
    row_count = gradients.shape[1]
    block_size = row_count * owners
    per_strip = gradients.shape[2] // (owners * block_size)
    half_width = block_size // 2
    side_bit = lax.axis_index("dp") % 2
    own_rows = gradients[0].reshape(row_count, owners, per_strip, block_size)
    doubled = jnp.repeat(own_rows, 2, axis=2)[None]
    spread = lax.all_to_all(doubled, "dp", split_axis=3, concat_axis=0, tiled=True)
    arrived = lax.all_to_all(spread, "fsdp", split_axis=2, concat_axis=1, tiled=True)
    blocks_in = arrived.reshape(arrived.shape[0], block_size, block_size)
    oriented = orient_blocks(blocks_in, side_bit)
    grams = jnp.einsum("gki,gkj->gij", oriented, oriented, preferred_element_type=jnp.float32)
    grams, blocks = (grams, blocks_in)
    stat_sum = jnp.sum(grams, axis=0)
    statistic = stat_sum / (groups * block_size)
    own_root = inverse_root(statistic).astype(jnp.bfloat16)
    partner = partner_2(own_root, "dp", 0)
    left_root = jnp.where(side_bit == 0, own_root, partner)
    right_root = jnp.where(side_bit == 0, partner, own_root)
    mean_grad = (jnp.sum(blocks, axis=0, dtype=jnp.float32) / groups).astype(jnp.bfloat16)
    right_half = lax.dynamic_slice_in_dim(right_root, side_bit * half_width, half_width, 1)
    right_part = jnp.dot(mean_grad, right_half, preferred_element_type=jnp.float32).astype(
        jnp.bfloat16
    )
    update_piece = jnp.dot(left_root, right_part, preferred_element_type=jnp.float32).astype(
        jnp.bfloat16
    )
    return lax.all_to_all(
        update_piece.reshape(block_size, 1, 1, half_width),
        "fsdp",
        split_axis=0,
        concat_axis=1,
        tiled=True,
    )


def solution(mesh):
    return jax.shard_map(
        per_device,
        mesh=mesh,
        in_specs=(P("dp", "fsdp", None),),
        out_specs=P("fsdp", None, "dp", None),
        check_vma=False,
    )
```

profile of v0, /device:TPU:32, one launch (start us, length us, event | category | flops | bytes accessed | tf_op | source)
XLA Modules:
  0.0 257.4 jit_solution(15626181009246141553)
XLA Ops:
  0.0 3.0 %reshape_squeeze.3 = bf16[16,32,4,512]{3,2,1,0:T(4,128)(2,1)S(1)} reshape(bf16[1,16,65536]{2,1,0:T(8,128)(2,1)} %param.1) | data formatting | bytes 4194304 | tf_op jit(solution)/shard_map/reshape;squeeze | solution.py:48
  3.0 1.2 copy.17
  4.2 0.6 broadcast_in_dim.7
  4.7 54.4 %all_to_all.51 = bf16[1,16,32,8,512]{4,1,2,0,3:T(8,128)(2,1)S(1)} all-to-all(bf16[1,16,32,8,512]{4,1,2,0,3:T(8,128)(2,1)S(1)} %bitcast.61), channel_id=1, replica_groups=mesh['dp'=8,'fsdp'=32] {'dp'}, dimensions={3} | all-to-all | bytes 8388608 | tf_op jit(solution)/shard_map/all_to_all | solution.py:50
  59.2 2.4 copy.18
  61.6 11.4 %all-to-all-start.1 = ((bf16[8,16,32,1,512]{4,1,0,3,2:T(8,128)(2,1)}), bf16[8,16,32,1,512]{4,1,0,3,2:T(8,128)(2,1)}, u32[]{:S(2)}, u32[]{:S(2)}) async-start(bf16[8,16,32,1,512]{4,1,0,3,2:T(8,128)(2,1)} %copy.18), calls=%async_computation.1 | async-start | bytes 8388608 | tf_op jit(solution)/shard_map/all_to_all | solution.py:51
  73.1 95.0 %all-to-all-done.1 = bf16[8,16,32,1,512]{4,1,0,3,2:T(8,128)(2,1)} async-done(((bf16[8,16,32,1,512]{4,1,0,3,2:T(8,128)(2,1)}), bf16[8,16,32,1,512]{4,1,0,3,2:T(8,128)(2,1)}, u32[]{:S(2)}, u32[]{:S(2)}) %all-to-all-start.1) | async-done | bytes 4194336 | tf_op jit(solution)/shard_map/all_to_all | solution.py:51
  168.1 4.8 %copy.19 = bf16[8,16,32,1,512]{4,1,2,0,3:T(8,128)(2,1)} copy(bf16[8,16,32,1,512]{4,1,0,3,2:T(8,128)(2,1)} %all-to-all-done.1) | data formatting | bytes 8388608 | tf_op jit(solution)/shard_map/all_to_all | solution.py:51
  172.9 7.0 %copy.20 = bf16[8,512,512]{1,2,0:T(8,128)(2,1)} copy(bf16[8,512,512]{2,1,0:T(8,128)(2,1)} %bitcast.59) | data formatting | bytes 8388608 | tf_op jit(solution)/shard_map/reshape | solution.py:52
  179.9 6.5 %select_reduce_fusion = (f32[]{:T(128)}, f32[512,512]{1,0:T(8,128)S(1)}) fusion(bf16[8,512,512]{2,1,0:T(8,128)(2,1)} %bitcast.60, bf16[8,512,512]{1,2,0:T(8,128)(2,1)} %copy.20, pred[]{:T(512)S(6)} %eq.26), kind=kOutput, calls=%fused_computation.25 | convolution fusion | flops 2150629376 | bytes 9437189 | tf_op jit(solution)/shard_map/gki,gkj->gij/dot_general | solution.py:54
  187.1 2.6 %fusion.29 = f32[512,512]{1,0:T(8,128)S(1)} fusion(f32[512,512]{1,0:T(8,128)S(1)} %get-tuple-element.6, f32[]{:T(128)} %get-tuple-element.5), kind=kOutput, calls=%fused_computation.35 | convolution fusion | flops 1611923456 | bytes 2097156 | tf_op jit(solution)/shard_map/dot_general | solution.py:24
  189.7 2.5 fusion.11
  192.2 1.8 fusion.102
  194.1 2.5 fusion.101
  196.6 1.9 fusion.25
  198.5 1.9 fusion.27
  200.4 2.0 fusion.103
  202.5 1.8 fusion.104
  204.3 1.9 fusion.21
  206.3 1.9 fusion.23
  208.2 1.8 fusion.105
  210.0 1.8 fusion.106
  211.9 1.9 fusion.17
  213.8 2.1 fusion.19
  216.0 1.8 fusion.107
  217.8 1.8 fusion.108
  219.7 1.9 fusion.13
  221.6 1.9 fusion.15
  223.5 1.8 fusion.109
  225.4 1.9 fusion.3
  227.2 2.1 convolution_convert_fusion
  229.3 2.5 collective-permute-start
  231.8 3.2 %convert_reduce_fusion = f32[32,16,512]{2,1,0:T(8,128)S(1)} fusion(bf16[8,16,32,1,512]{4,1,0,3,2:T(8,128)(2,1)} %all-to-all-done.1), kind=kLoop, calls=%fused_computation | loop fusion | flops 3932160 | bytes 5242880 | tf_op jit(solution)/shard_map/reduce_sum | solution.py:62
  234.9 0.1 multiply_convert_fusion
  235.1 0.0 collective-permute-done
  235.1 0.7 fusion.5
  235.9 0.5 broadcast.97
  236.4 0.8 reduce.1
  237.2 0.1 reshape.14
  237.2 18.7 %all_to_all.52 = bf16[32,2,2048]{2,1,0:T(2,128)(2,1)S(1)} all-to-all(bf16[32,2,2048]{2,1,0:T(2,128)(2,1)S(1)} %reshape.14), channel_id=1, replica_groups=mesh['dp'=8,'fsdp'=32] {'fsdp'}, dimensions={0} | all-to-all | bytes 524288 | tf_op jit(solution)/shard_map/all_to_all | solution.py:70
  256.0 0.3 reshape.15
  256.3 0.8 copy.23
  (1 shorter events, 0.0 us)
Async XLA Ops:
  61.6 106.5 %all-to-all-start.1 = ((bf16[8,16,32,1,512]{4,1,0,3,2:T(8,128)(2,1)}), bf16[8,16,32,1,512]{4,1,0,3,2:T(8,128)(2,1)}, u32[]{:S(2)}, u32[]{:S(2)}) async-start(bf16[8,16,32,1,512]{4,1,0,3,2:T(8,128)(2,1)} %copy.18), calls=%async_computation.1 | async-start | bytes 8388608 | tf_op jit(solution)/shard_map/all_to_all | solution.py:51
  229.3 5.8 %collective-permute-start = (bf16[512,512]{1,0:T(8,128)(2,1)S(1)}, bf16[512,512]{1,0:T(8,128)(2,1)S(1)}, u32[]{:S(2)}, u32[]{:S(2)}) collective-permute-start(bf16[512,512]{1,0:T(8,128)(2,1)S(1)} %convolution_convert_fusion), channel_id=1, source_target_pairs={{0,32},{32,0},{64,96},{96,64},{128,160},{160,128},{192,224},{224,1... | collective-permute-start | bytes 1572872 | tf_op jit(solution)/shard_map/ppermute | solution.py:10
where the time goes:
time: 261 us; the launch traced here: 257 us
  waiting for transfers between devices  95 us (36%)
  blocking collectives  73.2 us (28%)
  matrix products  49.3 us (19%)
  local copies, waits for them, and re-layouts  20.6 us (8%)
  starting transfers between devices  13.9 us (5%)
  other arithmetic  4.1 us (2%)
    all_to_all x1, waiting for transfers between devices, per_device(): lax.all_to_all(spread, 'fsdp', split_axis=2, concat_axis=1, tiled=True)  95 us
    all_to_all x1, blocking collectives, per_device(): lax.all_to_all(doubled, 'dp', split_axis=3, concat_axis=0, tiled=True)  54.4 us
    all_to_all x1, blocking collectives, per_device(): lax.all_to_all(update_piece.reshape(block_size, 1, 1, half_width), 'fsdp'...  18.7 us
    dot_general x6, matrix products, inverse_root(): jnp.dot(inverse, factor, precision=lax.Precision.HIGHEST, preferred_eleme...  12.5 us
    all_to_all x1, starting transfers between devices, per_device(): lax.all_to_all(spread, 'fsdp', split_axis=2, concat_axis=1, tiled=True)  11.4 us
    dot_general x5, matrix products, inverse_root(): jnp.dot(factor, factor, precision=lax.Precision.HIGHEST, preferred_elemen...  10.3 us
    dot_general x5, matrix products, inverse_root(): jnp.dot(fourth, moment, precision=lax.Precision.HIGHEST, preferred_elemen...  9.9 us
    dot_general x5, matrix products, inverse_root(): jnp.dot(square, square, precision=lax.Precision.HIGHEST, preferred_elemen...  9.4 us
  transfers between devices with their start and end apart: 2, of which 1 were waited for; matrix products, arithmetic and copies ran while one was open for 1% of the time, Pallas kernels for 0%

commit v1 on v0

v1 whole, which is shorter than its diff:
```python
import jax
import jax.numpy as jnp
from jax import lax
from jax.experimental import pallas as pl
from jax.experimental.pallas import tpu as pltpu
from jax.sharding import Mesh
from jax.sharding import PartitionSpec as P

ITERS = 6
GROUPS = 8
BLOCK = 512
PER_STRIP = 4
STRIPS = 32
HALF = 256
LANE = 128
STRIPS_PER_STEP = 8


def dot_nn(a, b):
    return lax.dot_general(a, b, (((1,), (0,)), ((), ())), preferred_element_type=jnp.float32)


def dot_nt(a, b):
    return lax.dot_general(a, b, (((1,), (1,)), ((), ())), preferred_element_type=jnp.float32)


def dot_tn(a, b):
    return lax.dot_general(a, b, (((0,), (0,)), ((), ())), preferred_element_type=jnp.float32)


def relayout_kernel(in_ref, out_ref):
    for strip in range(STRIPS_PER_STEP):
        for k in range(PER_STRIP):
            start = (strip * PER_STRIP + k) * BLOCK
            out_ref[k, strip] = in_ref[:, start : start + BLOCK]


def relayout(rows):
    width = STRIPS_PER_STEP * PER_STRIP * BLOCK
    return pl.pallas_call(
        relayout_kernel,
        grid=(STRIPS // STRIPS_PER_STEP,),
        in_specs=[pl.BlockSpec((16, width), lambda i: (0, i))],
        out_specs=pl.BlockSpec((PER_STRIP, STRIPS_PER_STEP, 16, BLOCK), lambda i: (0, i, 0, 0)),
        out_shape=jax.ShapeDtypeStruct((PER_STRIP, STRIPS, 16, BLOCK), jnp.bfloat16),
    )(rows)


def gram_kernel(side_ref, in_ref, keep_ref, send_ref, mean_ref):
    side = side_ref[0]
    group = pl.program_id(0)
    block = in_ref[0]
    left = dot_nt(block, block)
    right = dot_tn(block, block)
    own = jnp.where(side == 0, left, right)
    other = jnp.where(side == 0, right, left)
    wide = block.astype(jnp.float32)

    @pl.when(group == 0)
    def _():
        keep_ref[...] = own
        send_ref[...] = other
        mean_ref[...] = wide

    @pl.when(group > 0)
    def _():
        keep_ref[...] += own
        send_ref[...] += other
        mean_ref[...] += wide


def grams(side, blocks):
    square = jax.ShapeDtypeStruct((BLOCK, BLOCK), jnp.float32)
    whole = pl.BlockSpec((BLOCK, BLOCK), lambda i: (0, 0))
    return pl.pallas_call(
        gram_kernel,
        grid=(blocks.shape[0],),
        in_specs=[
            pl.BlockSpec(memory_space=pltpu.SMEM),
            pl.BlockSpec((1, BLOCK, BLOCK), lambda i: (i, 0, 0)),
        ],
        out_specs=[whole, whole, whole],
        out_shape=[square, square, square],
        compiler_params=pltpu.CompilerParams(vmem_limit_bytes=32 * 1024 * 1024),
    )(side, blocks)


def root_kernel(own_ref, other_ref, out_ref):
    row = lax.broadcasted_iota(jnp.int32, (BLOCK, BLOCK), 0)
    col = lax.broadcasted_iota(jnp.int32, (BLOCK, BLOCK), 1)
    diagonal = row == col
    stat = own_ref[...] + other_ref[...]
    trace = jnp.sum(jnp.where(diagonal, stat, 0.0), keepdims=True)
    f = stat * (0.2 / trace)
    y = f
    for iteration in range(ITERS):
        fb = f.astype(jnp.bfloat16)
        if iteration > 0:
            y = y + f - dot_nn(y.astype(jnp.bfloat16), fb)
        if iteration + 1 < ITERS:
            g = 2.0 * f - dot_nn(fb, fb)
            gb = g.astype(jnp.bfloat16)
            h = 2.0 * g - dot_nn(gb, gb)
            f = 1.25**4 * (f - dot_nn(h.astype(jnp.bfloat16), fb))
    scale = lax.rsqrt(jnp.sqrt(trace * (1.0 / (GROUPS * BLOCK)))) * 1.25**ITERS
    out_ref[...] = (scale * (jnp.where(diagonal, 1.0, 0.0) - y)).astype(jnp.bfloat16)


def inverse_root(own, other):
    return pl.pallas_call(
        root_kernel,
        out_shape=jax.ShapeDtypeStruct((BLOCK, BLOCK), jnp.bfloat16),
        compiler_params=pltpu.CompilerParams(vmem_limit_bytes=48 * 1024 * 1024),
        cost_estimate=pl.CostEstimate(
            flops=20 * 2 * BLOCK**3, bytes_accessed=10 * BLOCK * BLOCK, transcendentals=0
        ),
    )(own, other)


def update_kernel(side_ref, own_ref, other_ref, mean_own_ref, mean_other_ref, out_ref):
    side = side_ref[0]
    mean = ((mean_own_ref[...] + mean_other_ref[...]) * (1.0 / GROUPS)).astype(jnp.bfloat16)

    def piece(left_ref, right_ref, start):
        inner = dot_nn(mean, right_ref[:, start : start + HALF]).astype(jnp.bfloat16)
        out_ref[...] = dot_nn(left_ref[...], inner).astype(jnp.bfloat16)

    @pl.when(side == 0)
    def _():
        piece(own_ref, other_ref, 0)

    @pl.when(side == 1)
    def _():
        piece(other_ref, own_ref, HALF)


def update_piece(side, own, other, mean_own, mean_other):
    vmem = pl.BlockSpec(memory_space=pltpu.VMEM)
    return pl.pallas_call(
        update_kernel,
        in_specs=[pl.BlockSpec(memory_space=pltpu.SMEM), vmem, vmem, vmem, vmem],
        out_shape=jax.ShapeDtypeStruct((BLOCK, HALF), jnp.bfloat16),
        compiler_params=pltpu.CompilerParams(vmem_limit_bytes=32 * 1024 * 1024),
    )(side, own, other, mean_own, mean_other)


def swap_cores(x):
    return lax.ppermute(x, "core", [(0, 1), (1, 0)])


def per_device(gradients):
    side = lax.axis_index("core").astype(jnp.int32).reshape(1)
    send = relayout(gradients[0]).reshape(PER_STRIP * STRIPS, 16, BLOCK)
    arrived = lax.all_to_all(send, ("x", "y", "z"), split_axis=0, concat_axis=0, tiled=True)
    blocks = arrived.reshape(PER_STRIP, BLOCK, BLOCK)
    keep, other, mean_own = grams(side, blocks)
    stat_other = swap_cores(other)
    mean_other = swap_cores(mean_own)
    own_root = inverse_root(keep, stat_other)
    other_root = swap_cores(own_root)
    piece = update_piece(side, own_root, other_root, mean_own, mean_other)
    return lax.all_to_all(
        piece.reshape(BLOCK, 1, 1, HALF), ("y", "z"), split_axis=0, concat_axis=1, tiled=True
    )


def solution(mesh):
    fine = Mesh(mesh.devices.reshape(4, 2, 4, 8), ("x", "core", "y", "z"))
    return jax.shard_map(
        per_device,
        mesh=fine,
        in_specs=(P(("x", "core"), ("y", "z"), None),),
        out_specs=P(("y", "z"), None, ("x", "core"), None),
        check_vma=False,
    )
```

time: 261 us -> 109 us (0.42); the launches traced: 257 us -> 109 us
  blocking collectives: 73.2 us -> 17 us
  matrix products: 49.3 us -> 0 us
  waiting for transfers between devices: 95 us -> 57.7 us
  local copies, waits for them, and re-layouts: 20.6 us -> 1.67 us
  Pallas kernels: 0 us -> 15.5 us
  other arithmetic: 4.1 us -> 0.81 us
    all_to_all x2 -> x1, blocking collectives: 73.2 us -> 17 us  [per_device(): lax.all_to_all(piece.reshape(BLOCK, 1, 1, HALF), ('y', 'z'), split_axis=0...]
    dot_general x23 -> x0, matrix products: 49.3 us -> none  [the longest x6 12.5 us: inverse_root(): jnp.dot(inverse, factor, precision=lax.Precision.HIGHEST, preferred_eleme...]
    all_to_all x1, waiting for transfers between devices: 95 us -> 53.8 us  [per_device(): lax.all_to_all(send, ('x', 'y', 'z'), split_axis=0, concat_axis=0, tiled=...]
    pallas_call x0 -> x4, Pallas kernels: none -> 15.5 us  [the longest x1 6.73 us: inverse_root(): pl.pallas_call(root_kernel, out_shape=jax.ShapeDtypeStruct((BLOCK, BLOCK)...]
    all_to_all x3 -> x1, local copies, waits for them, and re-layouts: 8.01 us -> 0.78 us  [per_device(): lax.all_to_all(piece.reshape(BLOCK, 1, 1, HALF), ('y', 'z'), split_axis=0...]
    reshape x2 -> x1, local copies, waits for them, and re-layouts: 7.49 us -> 0.51 us  [per_device(): piece.reshape(BLOCK, 1, 1, HALF)]
    another operation x2 -> x0, local copies, waits for them, and re-layouts: 4.18 us -> none  [per_device(): own_rows = gradients[0].reshape(row_count, owners, per_strip, block_size)]
    ppermute x1 -> x3, waiting for transfers between devices: 0.01 us -> 3.92 us  [swap_cores(): return lax.ppermute(x, 'core', [(0, 1), (1, 0)])]
  transfers between devices with their start and end apart: 2 -> 4, of which waited for: 1 -> 3; matrix products, arithmetic and copies ran while one was open for 1% -> 0% of each run, Pallas kernels for 0% -> 6%
where the time goes in v1:
time: 109 us
  waiting for transfers between devices  57.7 us (53%)
  blocking collectives  17 us (16%)
  starting transfers between devices  15.8 us (14%)
  Pallas kernels  15.5 us (14%)
  local copies, waits for them, and re-layouts  1.67 us (2%)
    all_to_all x1, waiting for transfers between devices, per_device(): lax.all_to_all(send, ('x', 'y', 'z'), split_axis=0, concat_axis=0, tiled=...  53.8 us
    all_to_all x1, blocking collectives, per_device(): lax.all_to_all(piece.reshape(BLOCK, 1, 1, HALF), ('y', 'z'), split_axis=0...  17 us
    all_to_all x1, starting transfers between devices, per_device(): lax.all_to_all(send, ('x', 'y', 'z'), split_axis=0, concat_axis=0, tiled=...  15 us
    pallas_call x1, Pallas kernels, inverse_root(): pl.pallas_call(root_kernel, out_shape=jax.ShapeDtypeStruct((BLOCK, BLOCK)...  6.73 us
    pallas_call x1, Pallas kernels, grams(): pl.pallas_call(gram_kernel, grid=(blocks.shape[0],), in_specs=[pl.BlockSp...  4.13 us
    ppermute x3, waiting for transfers between devices, swap_cores(): return lax.ppermute(x, 'core', [(0, 1), (1, 0)])  3.92 us
    pallas_call x1, Pallas kernels, relayout(): pl.pallas_call(relayout_kernel, grid=(STRIPS // STRIPS_PER_STEP,), in_spe...  3.76 us
  transfers between devices with their start and end apart: 4, of which 3 were waited for; matrix products, arithmetic and copies ran while one was open for 0% of the time, Pallas kernels for 6%

profile of v1, /device:TPU:32, one launch (start us, length us, event | category | flops | bytes accessed | tf_op | source)
XLA Modules:
  0.0 108.7 jit_solution(13978877910042759219)
XLA Ops:
  0.0 3.8 %shard_map.17 = bf16[4,32,16,512]{3,2,1,0:T(8,128)(2,1)} custom-call(bf16[16,65536]{1,0:T(8,128)(2,1)} %bitcast.13), custom_call_target="tpu_custom_call" | custom-call | tf_op jit(solution)/shard_map/pallas_call | solution.py:40
  3.8 15.0 %all-to-all-start = ((bf16[128,16,512]{2,1,0:T(8,128)(2,1)}), bf16[128,16,512]{2,1,0:T(8,128)(2,1)S(1)}, u32[]{:S(2)}, u32[]{:S(2)}) async-start(bf16[128,16,512]{2,1,0:T(8,128)(2,1)} %bitcast.12), calls=%async_computation | async-start | bytes 4194304 | tf_op jit(solution)/shard_map/all_to_all | solution.py:154
  18.8 53.8 %all-to-all-done = bf16[128,16,512]{2,1,0:T(8,128)(2,1)S(1)} async-done(((bf16[128,16,512]{2,1,0:T(8,128)(2,1)}), bf16[128,16,512]{2,1,0:T(8,128)(2,1)S(1)}, u32[]{:S(2)}, u32[]{:S(2)}) %all-to-all-start) | async-done | bytes 2097184 | tf_op jit(solution)/shard_map/all_to_all | solution.py:154
  72.6 4.1 %shard_map.18 = (f32[512,512]{1,0:T(8,128)S(1)}, f32[512,512]{1,0:T(8,128)S(1)}, f32[512,512]{1,0:T(8,128)S(1)}) custom-call(s32[1]{0:T(128)} %bitcast.side_ref, bf16[4,512,512]{2,1,0:T(8,128)(2,1)S(1)} %bitcast.10), custom_call_target="tpu_custom_call" | custom-call | tf_op jit(solution)/shard_map/pallas_call | solution.py:75
  76.7 0.1 collective-permute-start
  76.8 0.5 collective-permute-start.2
  77.3 2.1 %collective-permute-done.other_ref = f32[512,512]{1,0:T(8,128)S(1)} collective-permute-done((f32[512,512]{1,0:T(8,128)S(1)}, f32[512,512]{1,0:T(8,128)S(1)}, u32[]{:S(2)}, u32[]{:S(2)}) %collective-permute-start) | collective-permute-done | bytes 1048608 | tf_op jit(solution)/shard_map/ppermute | solution.py:148
  79.5 6.7 %shard_map.19.own_ref = bf16[512,512]{1,0:T(8,128)(2,1)S(1)} custom-call(f32[512,512]{1,0:T(8,128)S(1)} %get-tuple-element.8.own_ref, f32[512,512]{1,0:T(8,128)S(1)} %collective-permute-done.other_ref), custom_call_target="tpu_custom_call" | custom-call | flops 5368709120 | bytes 2621440 | tf_op jit(solution)/shard_map/pallas_call | solution.py:110
  86.2 0.2 collective-permute-start.1
  86.5 0.0 collective-permute-done.2.mean_other_ref
  86.5 1.8 %collective-permute-done.1.other_ref = bf16[512,512]{1,0:T(8,128)(2,1)S(1)} collective-permute-done((bf16[512,512]{1,0:T(8,128)(2,1)S(1)}, bf16[512,512]{1,0:T(8,128)(2,1)S(1)}, u32[]{:S(2)}, u32[]{:S(2)}) %collective-permute-start.1) | collective-permute-done | bytes 524320 | tf_op jit(solution)/shard_map/ppermute | solution.py:148
  88.2 0.9 shard_map.20
  89.1 0.5 broadcast
  89.7 0.8 reduce
  90.5 0.1 reshape.16
  90.5 17.0 %all_to_all.23 = bf16[32,2,2048]{2,1,0:T(2,128)(2,1)S(1)} all-to-all(bf16[32,2,2048]{2,1,0:T(2,128)(2,1)S(1)} %reshape.16), channel_id=1, replica_groups=mesh['x'=4,'core'=2,'y'=4,'z'=8] {'y','z'}, dimensions={0} | all-to-all | bytes 524288 | tf_op jit(solution)/shard_map/all_to_all | solution.py:162
  107.6 0.3 reshape.17
  107.9 0.8 copy.6
  (1 shorter events, 0.0 us)
Async XLA Ops:
  3.8 68.8 %all-to-all-start = ((bf16[128,16,512]{2,1,0:T(8,128)(2,1)}), bf16[128,16,512]{2,1,0:T(8,128)(2,1)S(1)}, u32[]{:S(2)}, u32[]{:S(2)}) async-start(bf16[128,16,512]{2,1,0:T(8,128)(2,1)} %bitcast.12), calls=%async_computation | async-start | bytes 4194304 | tf_op jit(solution)/shard_map/all_to_all | solution.py:154
  76.7 2.7 %collective-permute-start = (f32[512,512]{1,0:T(8,128)S(1)}, f32[512,512]{1,0:T(8,128)S(1)}, u32[]{:S(2)}, u32[]{:S(2)}) collective-permute-start(f32[512,512]{1,0:T(8,128)S(1)} %get-tuple-element.9), channel_id=1, source_target_pairs={{0,32},{32,0},{1,33},{33,1},{2,34},{34,2},{3,35},{35,3},{4,36},{36... | collective-permute-start | bytes 3145736 | tf_op jit(solution)/shard_map/ppermute | solution.py:148
  76.8 9.6 %collective-permute-start.2 = (f32[512,512]{1,0:T(8,128)S(1)}, f32[512,512]{1,0:T(8,128)S(1)}, u32[]{:S(2)}, u32[]{:S(2)}) collective-permute-start(f32[512,512]{1,0:T(8,128)S(1)} %get-tuple-element.10.mean_own_ref), channel_id=1, source_target_pairs={{0,32},{32,0},{1,33},{33,1},{2,34},{34,2},{3,35},{35,3},{4,36},{36... | collective-permute-start | bytes 3145736 | tf_op jit(solution)/shard_map/ppermute | solution.py:148
  86.2 2.0 %collective-permute-start.1 = (bf16[512,512]{1,0:T(8,128)(2,1)S(1)}, bf16[512,512]{1,0:T(8,128)(2,1)S(1)}, u32[]{:S(2)}, u32[]{:S(2)}) collective-permute-start(bf16[512,512]{1,0:T(8,128)(2,1)S(1)} %shard_map.19.own_ref), channel_id=1, source_target_pairs={{0,32},{32,0},{1,33},{33,1},{2,34},{34,2},{3,35},{35,3},{4,36},{36... | collective-permute-start | bytes 1572872 | tf_op jit(solution)/shard_map/ppermute | solution.py:148

commit v2 on v1

v2 whole, which is shorter than its diff:
```python
import jax
import jax.numpy as jnp
from jax import lax
from jax.experimental import pallas as pl
from jax.experimental.pallas import tpu as pltpu
from jax.sharding import Mesh
from jax.sharding import PartitionSpec as P

ITERS = 6
GROUPS = 8
BLOCK = 512
PER_STRIP = 4
STRIPS = 32
HALF = 256
CHUNKS = 8
CHUNK = 8192


def dot_nn(a, b):
    return lax.dot_general(a, b, (((1,), (0,)), ((), ())), preferred_element_type=jnp.float32)


def dot_nt(a, b):
    return lax.dot_general(a, b, (((1,), (1,)), ((), ())), preferred_element_type=jnp.float32)


def dot_tn(a, b):
    return lax.dot_general(a, b, (((0,), (0,)), ((), ())), preferred_element_type=jnp.float32)


def relayout_kernel(in_ref, out_ref, landed, sems):
    copies = []
    for chunk in range(CHUNKS):
        columns = pl.ds(chunk * CHUNK, CHUNK)
        copies.append(
            pltpu.make_async_copy(in_ref.at[:, columns], landed.at[:, columns], sems.at[chunk])
        )
        copies[-1].start()
    for chunk in range(CHUNKS):
        copies[chunk].wait()
        for index in range(chunk * CHUNK // BLOCK, (chunk + 1) * CHUNK // BLOCK):
            strip, k = divmod(index, PER_STRIP)
            out_ref[k * STRIPS + strip] = landed[:, index * BLOCK : (index + 1) * BLOCK]


def relayout(rows):
    return pl.pallas_call(
        relayout_kernel,
        in_specs=[pl.BlockSpec(memory_space=pltpu.HBM)],
        out_specs=pl.BlockSpec(memory_space=pltpu.VMEM),
        out_shape=jax.ShapeDtypeStruct((PER_STRIP * STRIPS, 16, BLOCK), jnp.bfloat16),
        scratch_shapes=[
            pltpu.VMEM((16, STRIPS * PER_STRIP * BLOCK), jnp.bfloat16),
            pltpu.SemaphoreType.DMA((CHUNKS,)),
        ],
        compiler_params=pltpu.CompilerParams(vmem_limit_bytes=16 * 1024 * 1024),
    )(rows)


def left_gram(in_ref):
    wide = jnp.concatenate([in_ref[g] for g in range(PER_STRIP)], axis=1)
    return dot_nt(wide, wide)


def right_gram(in_ref):
    tall = in_ref[...].reshape(PER_STRIP * BLOCK, BLOCK)
    return dot_tn(tall, tall)


def send_kernel(side_ref, in_ref, send_ref):
    @pl.when(side_ref[0] == 0)
    def _():
        send_ref[...] = right_gram(in_ref)

    @pl.when(side_ref[0] == 1)
    def _():
        send_ref[...] = left_gram(in_ref)


def keep_kernel(side_ref, in_ref, keep_ref, mean_ref):
    @pl.when(side_ref[0] == 0)
    def _():
        keep_ref[...] = left_gram(in_ref)

    @pl.when(side_ref[0] == 1)
    def _():
        keep_ref[...] = right_gram(in_ref)

    total = in_ref[0].astype(jnp.float32)
    for group in range(1, PER_STRIP):
        total += in_ref[group].astype(jnp.float32)
    mean_ref[...] = total


def gram(kernel, n_out, side, blocks):
    square = jax.ShapeDtypeStruct((BLOCK, BLOCK), jnp.float32)
    return pl.pallas_call(
        kernel,
        in_specs=[
            pl.BlockSpec(memory_space=pltpu.SMEM),
            pl.BlockSpec(memory_space=pltpu.VMEM),
        ],
        out_shape=[square] * n_out,
        compiler_params=pltpu.CompilerParams(vmem_limit_bytes=32 * 1024 * 1024),
        cost_estimate=pl.CostEstimate(
            flops=4 * 2 * BLOCK**3, bytes_accessed=16 * BLOCK * BLOCK, transcendentals=0
        ),
    )(side, blocks)


def root_kernel(own_ref, other_ref, out_ref):
    row = lax.broadcasted_iota(jnp.int32, (BLOCK, BLOCK), 0)
    col = lax.broadcasted_iota(jnp.int32, (BLOCK, BLOCK), 1)
    diagonal = row == col
    stat = own_ref[...] + other_ref[...]
    trace = jnp.sum(jnp.where(diagonal, stat, 0.0), keepdims=True)
    growth = 1.25**4
    f = stat * (0.2 / trace)
    y = None
    for iteration in range(ITERS - 1):
        fb = f.astype(jnp.bfloat16)
        f_squared = dot_nn(fb, fb)
        g = 2.0 * f - f_squared
        gb = g.astype(jnp.bfloat16)
        h = 2.0 * g - dot_nn(gb, gb)
        hb = h.astype(jnp.bfloat16)
        if iteration + 2 < ITERS:
            y = f if y is None else y + f - dot_nn(y.astype(jnp.bfloat16), fb)
            f = growth * (f - dot_nn(hb, fb))
        else:
            af = f - f_squared
            w = f + growth * (af - dot_nn(hb, af.astype(jnp.bfloat16)))
            y = y + w - dot_nn(y.astype(jnp.bfloat16), w.astype(jnp.bfloat16))
    scale = lax.rsqrt(jnp.sqrt(trace * (1.0 / (GROUPS * BLOCK)))) * 1.25**ITERS
    out_ref[...] = (scale * (jnp.where(diagonal, 1.0, 0.0) - y)).astype(jnp.bfloat16)


def inverse_root(own, other):
    return pl.pallas_call(
        root_kernel,
        out_shape=jax.ShapeDtypeStruct((BLOCK, BLOCK), jnp.bfloat16),
        compiler_params=pltpu.CompilerParams(vmem_limit_bytes=48 * 1024 * 1024),
        cost_estimate=pl.CostEstimate(
            flops=20 * 2 * BLOCK**3, bytes_accessed=10 * BLOCK * BLOCK, transcendentals=0
        ),
    )(own, other)


def update_kernel(side_ref, own_ref, other_ref, mean_own_ref, mean_other_ref, out_ref):
    side = side_ref[0]
    mean = ((mean_own_ref[...] + mean_other_ref[...]) * (1.0 / GROUPS)).astype(jnp.bfloat16)

    def piece(left_ref, right_ref, start):
        inner = dot_nn(mean, right_ref[:, start : start + HALF]).astype(jnp.bfloat16)
        out_ref[...] = dot_nn(left_ref[...], inner).astype(jnp.bfloat16)

    @pl.when(side == 0)
    def _():
        piece(own_ref, other_ref, 0)

    @pl.when(side == 1)
    def _():
        piece(other_ref, own_ref, HALF)


def update_piece(side, own, other, mean_own, mean_other):
    vmem = pl.BlockSpec(memory_space=pltpu.VMEM)
    return pl.pallas_call(
        update_kernel,
        in_specs=[pl.BlockSpec(memory_space=pltpu.SMEM), vmem, vmem, vmem, vmem],
        out_shape=jax.ShapeDtypeStruct((BLOCK, HALF), jnp.bfloat16),
        compiler_params=pltpu.CompilerParams(vmem_limit_bytes=32 * 1024 * 1024),
    )(side, own, other, mean_own, mean_other)


def swap_cores(x):
    return lax.ppermute(x, "core", [(0, 1), (1, 0)])


def per_device(gradients):
    side = lax.axis_index("core").astype(jnp.int32).reshape(1)
    send = relayout(gradients[0])
    arrived = lax.all_to_all(send, ("x", "y", "z"), split_axis=0, concat_axis=0, tiled=True)
    blocks = arrived.reshape(PER_STRIP, BLOCK, BLOCK)
    (other,) = gram(send_kernel, 1, side, blocks)
    stat_other = swap_cores(other)
    keep, mean_own = gram(keep_kernel, 2, side, blocks)
    mean_other = swap_cores(mean_own)
    own_root = inverse_root(keep, stat_other)
    other_root = swap_cores(own_root)
    piece = update_piece(side, own_root, other_root, mean_own, mean_other)
    rows = lax.all_to_all(
        piece.reshape(STRIPS, 16, HALF), ("y", "z"), split_axis=0, concat_axis=0, tiled=True
    )
    return jnp.swapaxes(rows, 0, 1)[:, :, None, :]


def solution(mesh):
    fine = Mesh(mesh.devices.reshape(4, 2, 4, 8), ("x", "core", "y", "z"))
    return jax.shard_map(
        per_device,
        mesh=fine,
        in_specs=(P(("x", "core"), ("y", "z"), None),),
        out_specs=P(("y", "z"), None, ("x", "core"), None),
        check_vma=False,
    )
```

time: 109 us -> 104 us (0.954)
  Pallas kernels: 15.5 us -> 11.9 us
  waiting for transfers between devices: 57.7 us -> 56.1 us
    pallas_call x2 -> x3, Pallas kernels: 7.89 us -> 4.5 us  [the longest x2 2.78 us: gram(): pl.pallas_call(kernel, in_specs=[pl.BlockSpec(memory_space=pltpu.SMEM), p...]
    ppermute x3, waiting for transfers between devices: 3.92 us -> 2.32 us  [swap_cores(): return lax.ppermute(x, 'core', [(0, 1), (1, 0)])]
    unnamed x3 -> x2, local copies, waits for them, and re-layouts: 0.37 us -> 1.59 us
  transfers between devices with their start and end apart: 4 -> 4, of which waited for: 3 -> 3; matrix products, arithmetic and copies ran while one was open for 0% -> 0% of each run, Pallas kernels for 6% -> 8%
where the time goes in v2:
time: 104 us; the launch traced here: 103 us
  waiting for transfers between devices  56.1 us (54%)
  blocking collectives  17.1 us (16%)
  starting transfers between devices  15.9 us (15%)
  Pallas kernels  11.9 us (11%)
  local copies, waits for them, and re-layouts  2.37 us (2%)
    all_to_all x1, waiting for transfers between devices, per_device(): lax.all_to_all(send, ('x', 'y', 'z'), split_axis=0, concat_axis=0, tiled=...  53.8 us
    all_to_all x1, blocking collectives, per_device(): lax.all_to_all(piece.reshape(STRIPS, 16, HALF), ('y', 'z'), split_axis=0,...  17.1 us
    all_to_all x1, starting transfers between devices, per_device(): lax.all_to_all(send, ('x', 'y', 'z'), split_axis=0, concat_axis=0, tiled=...  15 us
    pallas_call x1, Pallas kernels, inverse_root(): pl.pallas_call(root_kernel, out_shape=jax.ShapeDtypeStruct((BLOCK, BLOCK)...  6.52 us
    pallas_call x2, Pallas kernels, gram(): pl.pallas_call(kernel, in_specs=[pl.BlockSpec(memory_space=pltpu.SMEM), p...  2.78 us
    ppermute x3, waiting for transfers between devices, swap_cores(): return lax.ppermute(x, 'core', [(0, 1), (1, 0)])  2.32 us
  transfers between devices with their start and end apart: 4, of which 3 were waited for; matrix products, arithmetic and copies ran while one was open for 0% of the time, Pallas kernels for 8%

profile of v2, /device:TPU:32, one launch (start us, length us, event | category | flops | bytes accessed | tf_op | source)
XLA Modules:
  0.0 103.5 jit_solution(634778738666715779)
XLA Ops:
  0.0 0.0 copy-start
  0.0 1.6 %copy-done = bf16[1,16,65536]{2,1,0:T(8,128)(2,1)S(1)} copy-done((bf16[1,16,65536]{2,1,0:T(8,128)(2,1)S(1)}, bf16[1,16,65536]{2,1,0:T(8,128)(2,1)}, u32[]{:S(2)}) %copy-start) | copy-done | bytes 2097176
  1.6 1.7 %shard_map.17 = bf16[128,16,512]{2,1,0:T(8,128)(2,1)} custom-call(bf16[16,65536]{1,0:T(8,128)(2,1)S(1)} %bitcast.7), custom_call_target="tpu_custom_call" | custom-call | tf_op jit(solution)/shard_map/pallas_call | solution.py:47
  3.3 15.0 %all-to-all-start = ((bf16[128,16,512]{2,1,0:T(8,128)(2,1)}), bf16[128,16,512]{2,1,0:T(8,128)(2,1)S(1)}, u32[]{:S(2)}, u32[]{:S(2)}) async-start(bf16[128,16,512]{2,1,0:T(8,128)(2,1)} %shard_map.17), calls=%async_computation | async-start | bytes 4194304 | tf_op jit(solution)/shard_map/all_to_all | solution.py:183
  18.3 53.8 %all-to-all-done = bf16[128,16,512]{2,1,0:T(8,128)(2,1)S(1)} async-done(((bf16[128,16,512]{2,1,0:T(8,128)(2,1)}), bf16[128,16,512]{2,1,0:T(8,128)(2,1)S(1)}, u32[]{:S(2)}, u32[]{:S(2)}) %all-to-all-start) | async-done | bytes 2097184 | tf_op jit(solution)/shard_map/all_to_all | solution.py:183
  72.2 1.3 %shard_map.19 = f32[512,512]{1,0:T(8,128)S(1)} custom-call(s32[1]{0:T(128)} %bitcast.side_ref, bf16[4,512,512]{2,1,0:T(8,128)(2,1)S(1)} %bitcast.8), custom_call_target="tpu_custom_call" | custom-call | flops 1073741824 | bytes 4194304 | tf_op jit(solution)/shard_map/pallas_call | solution.py:97
  73.4 0.1 collective-permute-start
  73.5 1.5 %shard_map.18 = (f32[512,512]{1,0:T(8,128)S(1)}, f32[512,512]{1,0:T(8,128)S(1)}) custom-call(s32[1]{0:T(128)} %bitcast.side_ref, bf16[4,512,512]{2,1,0:T(8,128)(2,1)S(1)} %bitcast.9), custom_call_target="tpu_custom_call" | custom-call | flops 1073741824 | bytes 4194304 | tf_op jit(solution)/shard_map/pallas_call | solution.py:97
  75.1 0.6 collective-permute-start.2
  75.6 0.5 collective-permute-done.other_ref
  76.2 6.5 %shard_map.20.own_ref = bf16[512,512]{1,0:T(8,128)(2,1)S(1)} custom-call(f32[512,512]{1,0:T(8,128)S(1)} %get-tuple-element.7.own_ref, f32[512,512]{1,0:T(8,128)S(1)} %collective-permute-done.other_ref), custom_call_target="tpu_custom_call" | custom-call | flops 5368709120 | bytes 2621440 | tf_op jit(solution)/shard_map/pallas_call | solution.py:139
  82.7 0.2 collective-permute-start.1
  82.9 0.0 collective-permute-done.2.mean_other_ref
  83.0 1.8 %collective-permute-done.1.other_ref = bf16[512,512]{1,0:T(8,128)(2,1)S(1)} collective-permute-done((bf16[512,512]{1,0:T(8,128)(2,1)S(1)}, bf16[512,512]{1,0:T(8,128)(2,1)S(1)}, u32[]{:S(2)}, u32[]{:S(2)}) %collective-permute-start.1) | collective-permute-done | bytes 524320 | tf_op jit(solution)/shard_map/ppermute | solution.py:177
  84.7 0.9 shard_map.21
  85.6 17.1 %all_to_all.10 = bf16[32,16,256]{2,1,0:T(8,128)(2,1)S(1)} all-to-all(bf16[32,16,256]{2,1,0:T(8,128)(2,1)S(1)} %bitcast.10), channel_id=1, replica_groups=mesh['x'=4,'core'=2,'y'=4,'z'=8] {'y','z'}, dimensions={0} | all-to-all | bytes 524288 | tf_op jit(solution)/shard_map/all_to_all | solution.py:192
  102.7 0.8 copy.3
Async XLA Ops:
  0.0 1.6 %copy-start = (bf16[1,16,65536]{2,1,0:T(8,128)(2,1)S(1)}, bf16[1,16,65536]{2,1,0:T(8,128)(2,1)}, u32[]{:S(2)}) copy-start(bf16[1,16,65536]{2,1,0:T(8,128)(2,1)} %param.1) | copy-start | bytes 6291460
  3.3 68.9 %all-to-all-start = ((bf16[128,16,512]{2,1,0:T(8,128)(2,1)}), bf16[128,16,512]{2,1,0:T(8,128)(2,1)S(1)}, u32[]{:S(2)}, u32[]{:S(2)}) async-start(bf16[128,16,512]{2,1,0:T(8,128)(2,1)} %shard_map.17), calls=%async_computation | async-start | bytes 4194304 | tf_op jit(solution)/shard_map/all_to_all | solution.py:183
  73.4 2.7 %collective-permute-start = (f32[512,512]{1,0:T(8,128)S(1)}, f32[512,512]{1,0:T(8,128)S(1)}, u32[]{:S(2)}, u32[]{:S(2)}) collective-permute-start(f32[512,512]{1,0:T(8,128)S(1)} %shard_map.19), channel_id=1, source_target_pairs={{0,32},{32,0},{1,33},{33,1},{2,34},{34,2},{3,35},{35,3},{4,36},{36... | collective-permute-start | bytes 3145736 | tf_op jit(solution)/shard_map/ppermute | solution.py:177
  75.1 7.9 %collective-permute-start.2 = (f32[512,512]{1,0:T(8,128)S(1)}, f32[512,512]{1,0:T(8,128)S(1)}, u32[]{:S(2)}, u32[]{:S(2)}) collective-permute-start(f32[512,512]{1,0:T(8,128)S(1)} %get-tuple-element.8.mean_own_ref), channel_id=1, source_target_pairs={{0,32},{32,0},{1,33},{33,1},{2,34},{34,2},{3,35},{35,3},{4,36},{36... | collective-permute-start | bytes 3145736 | tf_op jit(solution)/shard_map/ppermute | solution.py:177
  82.7 2.0 %collective-permute-start.1 = (bf16[512,512]{1,0:T(8,128)(2,1)S(1)}, bf16[512,512]{1,0:T(8,128)(2,1)S(1)}, u32[]{:S(2)}, u32[]{:S(2)}) collective-permute-start(bf16[512,512]{1,0:T(8,128)(2,1)S(1)} %shard_map.20.own_ref), channel_id=1, source_target_pairs={{0,32},{32,0},{1,33},{33,1},{2,34},{34,2},{3,35},{35,3},{4,36},{36... | collective-permute-start | bytes 1572872 | tf_op jit(solution)/shard_map/ppermute | solution.py:177

commit v3 on v2

--- a/solution.py
+++ b/solution.py
@@ -46,14 +46,14 @@
 def relayout(rows):
     return pl.pallas_call(
         relayout_kernel,
-        in_specs=[pl.BlockSpec(memory_space=pltpu.HBM)],
+        in_specs=[pl.BlockSpec(memory_space=pl.ANY)],
         out_specs=pl.BlockSpec(memory_space=pltpu.VMEM),
         out_shape=jax.ShapeDtypeStruct((PER_STRIP * STRIPS, 16, BLOCK), jnp.bfloat16),
         scratch_shapes=[
             pltpu.VMEM((16, STRIPS * PER_STRIP * BLOCK), jnp.bfloat16),
             pltpu.SemaphoreType.DMA((CHUNKS,)),
         ],
-        compiler_params=pltpu.CompilerParams(vmem_limit_bytes=16 * 1024 * 1024),
+        compiler_params=pltpu.CompilerParams(vmem_limit_bytes=50 * 1024 * 1024),
     )(rows)
 
 

time: 104 us -> 103 us (level)
  local copies, waits for them, and re-layouts: 2.37 us -> 0.78 us
  Pallas kernels: 11.9 us -> 13.1 us
    unnamed x2 -> x0, local copies, waits for them, and re-layouts: 1.59 us -> none
    pallas_call x1, Pallas kernels: 1.72 us -> 2.93 us  [relayout(): pl.pallas_call(relayout_kernel, in_specs=[pl.BlockSpec(memory_space=pl.AN...]
where the time goes in v3:
time: 103 us
  waiting for transfers between devices  56.1 us (54%)
  blocking collectives  17.1 us (17%)
  starting transfers between devices  15.9 us (15%)
  Pallas kernels  13.1 us (13%)
    all_to_all x1, waiting for transfers between devices, per_device(): lax.all_to_all(send, ('x', 'y', 'z'), split_axis=0, concat_axis=0, tiled=...  53.8 us
    all_to_all x1, blocking collectives, per_device(): lax.all_to_all(piece.reshape(STRIPS, 16, HALF), ('y', 'z'), split_axis=0,...  17.1 us
    all_to_all x1, starting transfers between devices, per_device(): lax.all_to_all(send, ('x', 'y', 'z'), split_axis=0, concat_axis=0, tiled=...  15 us
    pallas_call x1, Pallas kernels, inverse_root(): pl.pallas_call(root_kernel, out_shape=jax.ShapeDtypeStruct((BLOCK, BLOCK)...  6.52 us
    pallas_call x1, Pallas kernels, relayout(): pl.pallas_call(relayout_kernel, in_specs=[pl.BlockSpec(memory_space=pl.AN...  2.93 us
    pallas_call x2, Pallas kernels, gram(): pl.pallas_call(kernel, in_specs=[pl.BlockSpec(memory_space=pltpu.SMEM), p...  2.79 us
    ppermute x3, waiting for transfers between devices, swap_cores(): return lax.ppermute(x, 'core', [(0, 1), (1, 0)])  2.32 us
  transfers between devices with their start and end apart: 4, of which 3 were waited for; matrix products, arithmetic and copies ran while one was open for 0% of the time, Pallas kernels for 8%

profile of v3, /device:TPU:32, one launch (start us, length us, event | category | flops | bytes accessed | tf_op | source)
XLA Modules:
  0.0 103.1 jit_solution(7873146527208693182)
XLA Ops:
  0.0 2.9 %shard_map.17 = bf16[128,16,512]{2,1,0:T(8,128)(2,1)} custom-call(bf16[16,65536]{1,0:T(8,128)(2,1)} %bitcast.10), custom_call_target="tpu_custom_call" | custom-call | tf_op jit(solution)/shard_map/pallas_call | solution.py:47
  2.9 15.0 %all-to-all-start = ((bf16[128,16,512]{2,1,0:T(8,128)(2,1)}), bf16[128,16,512]{2,1,0:T(8,128)(2,1)S(1)}, u32[]{:S(2)}, u32[]{:S(2)}) async-start(bf16[128,16,512]{2,1,0:T(8,128)(2,1)} %shard_map.17), calls=%async_computation | async-start | bytes 4194304 | tf_op jit(solution)/shard_map/all_to_all | solution.py:183
  18.0 53.8 %all-to-all-done = bf16[128,16,512]{2,1,0:T(8,128)(2,1)S(1)} async-done(((bf16[128,16,512]{2,1,0:T(8,128)(2,1)}), bf16[128,16,512]{2,1,0:T(8,128)(2,1)S(1)}, u32[]{:S(2)}, u32[]{:S(2)}) %all-to-all-start) | async-done | bytes 2097184 | tf_op jit(solution)/shard_map/all_to_all | solution.py:183
  71.8 1.3 %shard_map.19 = f32[512,512]{1,0:T(8,128)S(1)} custom-call(s32[1]{0:T(128)} %bitcast.side_ref, bf16[4,512,512]{2,1,0:T(8,128)(2,1)S(1)} %bitcast.7), custom_call_target="tpu_custom_call" | custom-call | flops 1073741824 | bytes 4194304 | tf_op jit(solution)/shard_map/pallas_call | solution.py:97
  73.1 0.1 collective-permute-start
  73.2 1.5 %shard_map.18 = (f32[512,512]{1,0:T(8,128)S(1)}, f32[512,512]{1,0:T(8,128)S(1)}) custom-call(s32[1]{0:T(128)} %bitcast.side_ref, bf16[4,512,512]{2,1,0:T(8,128)(2,1)S(1)} %bitcast.8), custom_call_target="tpu_custom_call" | custom-call | flops 1073741824 | bytes 4194304 | tf_op jit(solution)/shard_map/pallas_call | solution.py:97
  74.7 0.6 collective-permute-start.2
  75.3 0.5 collective-permute-done.other_ref
  75.8 6.5 %shard_map.20.own_ref = bf16[512,512]{1,0:T(8,128)(2,1)S(1)} custom-call(f32[512,512]{1,0:T(8,128)S(1)} %get-tuple-element.7.own_ref, f32[512,512]{1,0:T(8,128)S(1)} %collective-permute-done.other_ref), custom_call_target="tpu_custom_call" | custom-call | flops 5368709120 | bytes 2621440 | tf_op jit(solution)/shard_map/pallas_call | solution.py:139
  82.3 0.2 collective-permute-start.1
  82.6 0.0 collective-permute-done.2.mean_other_ref
  82.6 1.8 %collective-permute-done.1.other_ref = bf16[512,512]{1,0:T(8,128)(2,1)S(1)} collective-permute-done((bf16[512,512]{1,0:T(8,128)(2,1)S(1)}, bf16[512,512]{1,0:T(8,128)(2,1)S(1)}, u32[]{:S(2)}, u32[]{:S(2)}) %collective-permute-start.1) | collective-permute-done | bytes 524320 | tf_op jit(solution)/shard_map/ppermute | solution.py:177
  84.3 0.9 shard_map.21
  85.3 17.1 %all_to_all.10 = bf16[32,16,256]{2,1,0:T(8,128)(2,1)S(1)} all-to-all(bf16[32,16,256]{2,1,0:T(8,128)(2,1)S(1)} %bitcast.9), channel_id=1, replica_groups=mesh['x'=4,'core'=2,'y'=4,'z'=8] {'y','z'}, dimensions={0} | all-to-all | bytes 524288 | tf_op jit(solution)/shard_map/all_to_all | solution.py:192
  102.3 0.8 copy.3
Async XLA Ops:
  2.9 68.9 %all-to-all-start = ((bf16[128,16,512]{2,1,0:T(8,128)(2,1)}), bf16[128,16,512]{2,1,0:T(8,128)(2,1)S(1)}, u32[]{:S(2)}, u32[]{:S(2)}) async-start(bf16[128,16,512]{2,1,0:T(8,128)(2,1)} %shard_map.17), calls=%async_computation | async-start | bytes 4194304 | tf_op jit(solution)/shard_map/all_to_all | solution.py:183
  73.1 2.7 %collective-permute-start = (f32[512,512]{1,0:T(8,128)S(1)}, f32[512,512]{1,0:T(8,128)S(1)}, u32[]{:S(2)}, u32[]{:S(2)}) collective-permute-start(f32[512,512]{1,0:T(8,128)S(1)} %shard_map.19), channel_id=1, source_target_pairs={{0,32},{32,0},{1,33},{33,1},{2,34},{34,2},{3,35},{35,3},{4,36},{36... | collective-permute-start | bytes 3145736 | tf_op jit(solution)/shard_map/ppermute | solution.py:177
  74.7 7.9 %collective-permute-start.2 = (f32[512,512]{1,0:T(8,128)S(1)}, f32[512,512]{1,0:T(8,128)S(1)}, u32[]{:S(2)}, u32[]{:S(2)}) collective-permute-start(f32[512,512]{1,0:T(8,128)S(1)} %get-tuple-element.8.mean_own_ref), channel_id=1, source_target_pairs={{0,32},{32,0},{1,33},{33,1},{2,34},{34,2},{3,35},{35,3},{4,36},{36... | collective-permute-start | bytes 3145736 | tf_op jit(solution)/shard_map/ppermute | solution.py:177
  82.3 2.0 %collective-permute-start.1 = (bf16[512,512]{1,0:T(8,128)(2,1)S(1)}, bf16[512,512]{1,0:T(8,128)(2,1)S(1)}, u32[]{:S(2)}, u32[]{:S(2)}) collective-permute-start(bf16[512,512]{1,0:T(8,128)(2,1)S(1)} %shard_map.20.own_ref), channel_id=1, source_target_pairs={{0,32},{32,0},{1,33},{33,1},{2,34},{34,2},{3,35},{35,3},{4,36},{36... | collective-permute-start | bytes 1572872 | tf_op jit(solution)/shard_map/ppermute | solution.py:177

commit v4 on v3

--- a/solution.py
+++ b/solution.py
@@ -67,22 +67,26 @@
     return dot_tn(tall, tall)
 
 
-def send_kernel(side_ref, in_ref, send_ref):
-    @pl.when(side_ref[0] == 0)
+def send_kernel(in_ref, send_ref):
+    side = lax.axis_index("core")
+
+    @pl.when(side == 0)
     def _():
         send_ref[...] = right_gram(in_ref)
 
-    @pl.when(side_ref[0] == 1)
+    @pl.when(side == 1)
     def _():
         send_ref[...] = left_gram(in_ref)
 
 
-def keep_kernel(side_ref, in_ref, keep_ref, mean_ref):
-    @pl.when(side_ref[0] == 0)
+def keep_kernel(in_ref, keep_ref, mean_ref):
+    side = lax.axis_index("core")
+
+    @pl.when(side == 0)
     def _():
         keep_ref[...] = left_gram(in_ref)
 
-    @pl.when(side_ref[0] == 1)
+    @pl.when(side == 1)
     def _():
         keep_ref[...] = right_gram(in_ref)
 
@@ -92,20 +96,16 @@
     mean_ref[...] = total
 
 
-def gram(kernel, n_out, side, blocks):
+def gram(kernel, n_out, blocks):
     square = jax.ShapeDtypeStruct((BLOCK, BLOCK), jnp.float32)
     return pl.pallas_call(
         kernel,
-        in_specs=[
-            pl.BlockSpec(memory_space=pltpu.SMEM),
-            pl.BlockSpec(memory_space=pltpu.VMEM),
-        ],
         out_shape=[square] * n_out,
         compiler_params=pltpu.CompilerParams(vmem_limit_bytes=32 * 1024 * 1024),
         cost_estimate=pl.CostEstimate(
             flops=4 * 2 * BLOCK**3, bytes_accessed=16 * BLOCK * BLOCK, transcendentals=0
         ),
-    )(side, blocks)
+    )(blocks)
 
 
 def root_kernel(own_ref, other_ref, out_ref):
@@ -146,8 +146,8 @@
     )(own, other)
 
 
-def update_kernel(side_ref, own_ref, other_ref, mean_own_ref, mean_other_ref, out_ref):
-    side = side_ref[0]
+def update_kernel(own_ref, other_ref, mean_own_ref, mean_other_ref, out_ref):
+    side = lax.axis_index("core")
     mean = ((mean_own_ref[...] + mean_other_ref[...]) * (1.0 / GROUPS)).astype(jnp.bfloat16)
 
     def piece(left_ref, right_ref, start):
@@ -163,14 +163,12 @@
         piece(other_ref, own_ref, HALF)
 
 
-def update_piece(side, own, other, mean_own, mean_other):
-    vmem = pl.BlockSpec(memory_space=pltpu.VMEM)
+def update_piece(own, other, mean_own, mean_other):
     return pl.pallas_call(
         update_kernel,
-        in_specs=[pl.BlockSpec(memory_space=pltpu.SMEM), vmem, vmem, vmem, vmem],
         out_shape=jax.ShapeDtypeStruct((BLOCK, HALF), jnp.bfloat16),
         compiler_params=pltpu.CompilerParams(vmem_limit_bytes=32 * 1024 * 1024),
-    )(side, own, other, mean_own, mean_other)
+    )(own, other, mean_own, mean_other)
 
 
 def swap_cores(x):
@@ -178,17 +176,16 @@
 
 
 def per_device(gradients):
-    side = lax.axis_index("core").astype(jnp.int32).reshape(1)
     send = relayout(gradients[0])
     arrived = lax.all_to_all(send, ("x", "y", "z"), split_axis=0, concat_axis=0, tiled=True)
     blocks = arrived.reshape(PER_STRIP, BLOCK, BLOCK)
-    (other,) = gram(send_kernel, 1, side, blocks)
+    (other,) = gram(send_kernel, 1, blocks)
     stat_other = swap_cores(other)
-    keep, mean_own = gram(keep_kernel, 2, side, blocks)
+    keep, mean_own = gram(keep_kernel, 2, blocks)
     mean_other = swap_cores(mean_own)
     own_root = inverse_root(keep, stat_other)
     other_root = swap_cores(own_root)
-    piece = update_piece(side, own_root, other_root, mean_own, mean_other)
+    piece = update_piece(own_root, other_root, mean_own, mean_other)
     rows = lax.all_to_all(
         piece.reshape(STRIPS, 16, HALF), ("y", "z"), split_axis=0, concat_axis=0, tiled=True
     )

time: 103 us -> 102 us (level)
  blocking collectives: 17.1 us -> 85.7 us
  waiting for transfers between devices: 56.1 us -> 2.32 us
  starting transfers between devices: 15.9 us -> 0.87 us
  Pallas kernels: 13.1 us -> 11.8 us
    all_to_all x0 -> x1, blocking collectives: none -> 68.6 us  [per_device(): lax.all_to_all(send, ('x', 'y', 'z'), split_axis=0, concat_axis=0, tiled=...]
    all_to_all x1 -> x0, waiting for transfers between devices: 53.8 us -> none  [per_device(): lax.all_to_all(send, ('x', 'y', 'z'), split_axis=0, concat_axis=0, tiled=...]
    all_to_all x1 -> x0, starting transfers between devices: 15 us -> none  [per_device(): lax.all_to_all(send, ('x', 'y', 'z'), split_axis=0, concat_axis=0, tiled=...]
    pallas_call x1, Pallas kernels: 2.93 us -> 1.59 us  [relayout(): pl.pallas_call(relayout_kernel, in_specs=[pl.BlockSpec(memory_space=pl.AN...]
  transfers between devices with their start and end apart: 4 -> 3, of which waited for: 3 -> 2; matrix products, arithmetic and copies ran while one was open for 0% -> 0% of each run, Pallas kernels for 8% -> 8%
where the time goes in v4:
time: 102 us
  blocking collectives  85.7 us (84%)
  Pallas kernels  11.8 us (12%)
  waiting for transfers between devices  2.32 us (2%)
    all_to_all x1, blocking collectives, per_device(): lax.all_to_all(send, ('x', 'y', 'z'), split_axis=0, concat_axis=0, tiled=...  68.6 us
    all_to_all x1, blocking collectives, per_device(): lax.all_to_all(piece.reshape(STRIPS, 16, HALF), ('y', 'z'), split_axis=0,...  17 us
    pallas_call x1, Pallas kernels, inverse_root(): pl.pallas_call(root_kernel, out_shape=jax.ShapeDtypeStruct((BLOCK, BLOCK)...  6.53 us
    pallas_call x2, Pallas kernels, gram(): pl.pallas_call(kernel, out_shape=[square] * n_out, compiler_params=pltpu....  2.8 us
    ppermute x3, waiting for transfers between devices, swap_cores(): return lax.ppermute(x, 'core', [(0, 1), (1, 0)])  2.32 us
  transfers between devices with their start and end apart: 3, of which 2 were waited for; matrix products, arithmetic and copies ran while one was open for 0% of the time, Pallas kernels for 8%

profile of v4, /device:TPU:32, one launch (start us, length us, event | category | flops | bytes accessed | tf_op | source)
XLA Modules:
  0.0 101.5 jit_solution(17338519443397449097)
XLA Ops:
  0.0 1.6 %shard_map.17 = bf16[128,16,512]{2,1,0:T(8,128)(2,1)S(1)} custom-call(bf16[16,65536]{1,0:T(8,128)(2,1)} %bitcast.9), custom_call_target="tpu_custom_call" | custom-call | tf_op jit(solution)/shard_map/pallas_call | solution.py:47
  1.6 68.6 %all_to_all.10 = bf16[128,16,512]{2,1,0:T(8,128)(2,1)S(1)} all-to-all(bf16[128,16,512]{2,1,0:T(8,128)(2,1)S(1)} %shard_map.17), channel_id=1, replica_groups=mesh['x'=4,'core'=2,'y'=4,'z'=8] {'x','y','z'}, dimensions={0} | all-to-all | bytes 4194304 | tf_op jit(solution)/shard_map/all_to_all | solution.py:180
  70.2 1.3 %shard_map.19 = f32[512,512]{1,0:T(8,128)S(1)} custom-call(bf16[4,512,512]{2,1,0:T(8,128)(2,1)S(1)} %bitcast.6), custom_call_target="tpu_custom_call" | custom-call | flops 1073741824 | bytes 4194304 | tf_op jit(solution)/shard_map/pallas_call | solution.py:101
  71.5 0.1 collective-permute-start
  71.6 1.5 %shard_map.18 = (f32[512,512]{1,0:T(8,128)S(1)}, f32[512,512]{1,0:T(8,128)S(1)}) custom-call(bf16[4,512,512]{2,1,0:T(8,128)(2,1)S(1)} %bitcast.7), custom_call_target="tpu_custom_call" | custom-call | flops 1073741824 | bytes 4194304 | tf_op jit(solution)/shard_map/pallas_call | solution.py:101
  73.1 0.6 collective-permute-start.2
  73.7 0.5 collective-permute-done.other_ref
  74.3 6.5 %shard_map.20.own_ref = bf16[512,512]{1,0:T(8,128)(2,1)S(1)} custom-call(f32[512,512]{1,0:T(8,128)S(1)} %get-tuple-element.7.own_ref, f32[512,512]{1,0:T(8,128)S(1)} %collective-permute-done.other_ref), custom_call_target="tpu_custom_call" | custom-call | flops 5368709120 | bytes 2621440 | tf_op jit(solution)/shard_map/pallas_call | solution.py:139
  80.8 0.2 collective-permute-start.1
  81.0 0.0 collective-permute-done.2.mean_other_ref
  81.0 1.8 %collective-permute-done.1.other_ref = bf16[512,512]{1,0:T(8,128)(2,1)S(1)} collective-permute-done((bf16[512,512]{1,0:T(8,128)(2,1)S(1)}, bf16[512,512]{1,0:T(8,128)(2,1)S(1)}, u32[]{:S(2)}, u32[]{:S(2)}) %collective-permute-start.1) | collective-permute-done | bytes 524320 | tf_op jit(solution)/shard_map/ppermute | solution.py:175
  82.8 0.9 shard_map.21
  83.7 17.0 %all_to_all.11 = bf16[32,16,256]{2,1,0:T(8,128)(2,1)S(1)} all-to-all(bf16[32,16,256]{2,1,0:T(8,128)(2,1)S(1)} %bitcast.8), channel_id=1, replica_groups=mesh['x'=4,'core'=2,'y'=4,'z'=8] {'y','z'}, dimensions={0} | all-to-all | bytes 524288 | tf_op jit(solution)/shard_map/all_to_all | solution.py:189
  100.8 0.8 copy.3
Async XLA Ops:
  71.5 2.7 %collective-permute-start = (f32[512,512]{1,0:T(8,128)S(1)}, f32[512,512]{1,0:T(8,128)S(1)}, u32[]{:S(2)}, u32[]{:S(2)}) collective-permute-start(f32[512,512]{1,0:T(8,128)S(1)} %shard_map.19), channel_id=1, source_target_pairs={{0,32},{32,0},{1,33},{33,1},{2,34},{34,2},{3,35},{35,3},{4,36},{36... | collective-permute-start | bytes 3145736 | tf_op jit(solution)/shard_map/ppermute | solution.py:175
  73.1 7.9 %collective-permute-start.2 = (f32[512,512]{1,0:T(8,128)S(1)}, f32[512,512]{1,0:T(8,128)S(1)}, u32[]{:S(2)}, u32[]{:S(2)}) collective-permute-start(f32[512,512]{1,0:T(8,128)S(1)} %get-tuple-element.8.mean_own_ref), channel_id=1, source_target_pairs={{0,32},{32,0},{1,33},{33,1},{2,34},{34,2},{3,35},{35,3},{4,36},{36... | collective-permute-start | bytes 3145736 | tf_op jit(solution)/shard_map/ppermute | solution.py:175
  80.8 2.0 %collective-permute-start.1 = (bf16[512,512]{1,0:T(8,128)(2,1)S(1)}, bf16[512,512]{1,0:T(8,128)(2,1)S(1)}, u32[]{:S(2)}, u32[]{:S(2)}) collective-permute-start(bf16[512,512]{1,0:T(8,128)(2,1)S(1)} %shard_map.20.own_ref), channel_id=1, source_target_pairs={{0,32},{32,0},{1,33},{33,1},{2,34},{34,2},{3,35},{35,3},{4,36},{36... | collective-permute-start | bytes 1572872 | tf_op jit(solution)/shard_map/ppermute | solution.py:175

commit v5 on v4

--- a/solution.py
+++ b/solution.py
@@ -12,6 +12,7 @@
 PER_STRIP = 4
 STRIPS = 32
 HALF = 256
+QUARTER = 128
 CHUNKS = 8
 CHUNK = 8192
 
@@ -57,14 +58,22 @@
     )(rows)
 
 
-def left_gram(in_ref):
+def left_gram(in_ref, out_ref):
     wide = jnp.concatenate([in_ref[g] for g in range(PER_STRIP)], axis=1)
-    return dot_nt(wide, wide)
-
-
-def right_gram(in_ref):
+    low = wide[HALF:]
+    store_gram(dot_nt(wide[:HALF], wide), dot_nt(low, low), out_ref)
+
+
+def right_gram(in_ref, out_ref):
     tall = in_ref[...].reshape(PER_STRIP * BLOCK, BLOCK)
-    return dot_tn(tall, tall)
+    low = tall[:, HALF:]
+    store_gram(dot_tn(tall[:, :HALF], tall), dot_tn(low, low), out_ref)
+
+
+def store_gram(top, corner, out_ref):
+    out_ref[:HALF] = top
+    out_ref[HALF:, :HALF] = corner[:QUARTER]
+    out_ref[HALF:, HALF:] = corner[QUARTER:]
 
 
 def send_kernel(in_ref, send_ref):
@@ -72,11 +81,11 @@
 
     @pl.when(side == 0)
     def _():
-        send_ref[...] = right_gram(in_ref)
+        right_gram(in_ref, send_ref)
 
     @pl.when(side == 1)
     def _():
-        send_ref[...] = left_gram(in_ref)
+        left_gram(in_ref, send_ref)
 
 
 def keep_kernel(in_ref, keep_ref, mean_ref):
@@ -84,11 +93,11 @@
 
     @pl.when(side == 0)
     def _():
-        keep_ref[...] = left_gram(in_ref)
+        left_gram(in_ref, keep_ref)
 
     @pl.when(side == 1)
     def _():
-        keep_ref[...] = right_gram(in_ref)
+        right_gram(in_ref, keep_ref)
 
     total = in_ref[0].astype(jnp.float32)
     for group in range(1, PER_STRIP):
@@ -96,11 +105,10 @@
     mean_ref[...] = total
 
 
-def gram(kernel, n_out, blocks):
-    square = jax.ShapeDtypeStruct((BLOCK, BLOCK), jnp.float32)
+def gram(kernel, rows, blocks):
     return pl.pallas_call(
         kernel,
-        out_shape=[square] * n_out,
+        out_shape=[jax.ShapeDtypeStruct((n, BLOCK), jnp.float32) for n in rows],
         compiler_params=pltpu.CompilerParams(vmem_limit_bytes=32 * 1024 * 1024),
         cost_estimate=pl.CostEstimate(
             flops=4 * 2 * BLOCK**3, bytes_accessed=16 * BLOCK * BLOCK, transcendentals=0
@@ -112,7 +120,10 @@
     row = lax.broadcasted_iota(jnp.int32, (BLOCK, BLOCK), 0)
     col = lax.broadcasted_iota(jnp.int32, (BLOCK, BLOCK), 1)
     diagonal = row == col
-    stat = own_ref[...] + other_ref[...]
+    packed = own_ref[...] + other_ref[...]
+    low = jnp.concatenate([packed[HALF:, :HALF], packed[HALF:, HALF:]], axis=0)
+    low = jnp.concatenate([packed[:HALF, HALF:].T, low], axis=1)
+    stat = jnp.concatenate([packed[:HALF], low], axis=0)
     trace = jnp.sum(jnp.where(diagonal, stat, 0.0), keepdims=True)
     growth = 1.25**4
     f = stat * (0.2 / trace)
@@ -146,12 +157,27 @@
     )(own, other)
 
 
-def update_kernel(own_ref, other_ref, mean_own_ref, mean_other_ref, out_ref):
+def mean_kernel(own_ref, other_ref, out_ref):
+    out_ref[...] = ((own_ref[...] + other_ref[...]) * (1.0 / GROUPS)).astype(jnp.bfloat16)
+
+
+def mean_block(own, other):
+    return pl.pallas_call(
+        mean_kernel,
+        out_shape=jax.ShapeDtypeStruct((BLOCK, BLOCK), jnp.bfloat16),
+        compiler_params=pltpu.CompilerParams(vmem_limit_bytes=16 * 1024 * 1024),
+        cost_estimate=pl.CostEstimate(
+            flops=2 * BLOCK * BLOCK, bytes_accessed=10 * BLOCK * BLOCK, transcendentals=0
+        ),
+    )(own, other)
+
+
+def update_kernel(own_ref, other_ref, mean_ref, out_ref):
     side = lax.axis_index("core")
-    mean = ((mean_own_ref[...] + mean_other_ref[...]) * (1.0 / GROUPS)).astype(jnp.bfloat16)
 
     def piece(left_ref, right_ref, start):
-        inner = dot_nn(mean, right_ref[:, start : start + HALF]).astype(jnp.bfloat16)
+        right = right_ref[:, start : start + HALF]
+        inner = dot_nn(mean_ref[...], right).astype(jnp.bfloat16)
         out_ref[...] = dot_nn(left_ref[...], inner).astype(jnp.bfloat16)
 
     @pl.when(side == 0)
@@ -163,12 +189,12 @@
         piece(other_ref, own_ref, HALF)
 
 
-def update_piece(own, other, mean_own, mean_other):
+def update_piece(own, other, mean):
     return pl.pallas_call(
         update_kernel,
         out_shape=jax.ShapeDtypeStruct((BLOCK, HALF), jnp.bfloat16),
         compiler_params=pltpu.CompilerParams(vmem_limit_bytes=32 * 1024 * 1024),
-    )(own, other, mean_own, mean_other)
+    )(own, other, mean)
 
 
 def swap_cores(x):
@@ -179,13 +205,13 @@
     send = relayout(gradients[0])
     arrived = lax.all_to_all(send, ("x", "y", "z"), split_axis=0, concat_axis=0, tiled=True)
     blocks = arrived.reshape(PER_STRIP, BLOCK, BLOCK)
-    (other,) = gram(send_kernel, 1, blocks)
+    (other,) = gram(send_kernel, (HALF + QUARTER,), blocks)
     stat_other = swap_cores(other)
-    keep, mean_own = gram(keep_kernel, 2, blocks)
+    keep, mean_own = gram(keep_kernel, (HALF + QUARTER, BLOCK), blocks)
     mean_other = swap_cores(mean_own)
     own_root = inverse_root(keep, stat_other)
     other_root = swap_cores(own_root)
-    piece = update_piece(own_root, other_root, mean_own, mean_other)
+    piece = update_piece(own_root, other_root, mean_block(mean_own, mean_other))
     rows = lax.all_to_all(
         piece.reshape(STRIPS, 16, HALF), ("y", "z"), split_axis=0, concat_axis=0, tiled=True
     )

time: 102 us -> 101 us (level)
    pallas_call x2 -> x3, Pallas kernels: 2.8 us -> 2.37 us  [the longest x2 2.28 us: gram(): pl.pallas_call(kernel, out_shape=[jax.ShapeDtypeStruct((n, BLOCK), jnp.fl...]
where the time goes in v5:
time: 101 us
  blocking collectives  85.7 us (85%)
  Pallas kernels  11.2 us (11%)
  waiting for transfers between devices  2.11 us (2%)
    all_to_all x1, blocking collectives, per_device(): lax.all_to_all(send, ('x', 'y', 'z'), split_axis=0, concat_axis=0, tiled=...  68.6 us
    all_to_all x1, blocking collectives, per_device(): lax.all_to_all(piece.reshape(STRIPS, 16, HALF), ('y', 'z'), split_axis=0,...  17.1 us
    pallas_call x1, Pallas kernels, inverse_root(): pl.pallas_call(root_kernel, out_shape=jax.ShapeDtypeStruct((BLOCK, BLOCK)...  6.47 us
    pallas_call x2, Pallas kernels, gram(): pl.pallas_call(kernel, out_shape=[jax.ShapeDtypeStruct((n, BLOCK), jnp.fl...  2.28 us
    ppermute x3, waiting for transfers between devices, swap_cores(): return lax.ppermute(x, 'core', [(0, 1), (1, 0)])  2.11 us
  transfers between devices with their start and end apart: 3, of which 2 were waited for; matrix products, arithmetic and copies ran while one was open for 0% of the time, Pallas kernels for 8%

profile of v5, /device:TPU:32, one launch (start us, length us, event | category | flops | bytes accessed | tf_op | source)
XLA Modules:
  0.0 100.7 jit_solution(2585975404830171810)
XLA Ops:
  0.0 1.6 %shard_map.17 = bf16[128,16,512]{2,1,0:T(8,128)(2,1)S(1)} custom-call(bf16[16,65536]{1,0:T(8,128)(2,1)} %bitcast.9), custom_call_target="tpu_custom_call" | custom-call | tf_op jit(solution)/shard_map/pallas_call | solution.py:48
  1.6 68.6 %all_to_all.10 = bf16[128,16,512]{2,1,0:T(8,128)(2,1)S(1)} all-to-all(bf16[128,16,512]{2,1,0:T(8,128)(2,1)S(1)} %shard_map.17), channel_id=1, replica_groups=mesh['x'=4,'core'=2,'y'=4,'z'=8] {'x','y','z'}, dimensions={0} | all-to-all | bytes 4194304 | tf_op jit(solution)/shard_map/all_to_all | solution.py:206
  70.2 1.0 %shard_map.19 = f32[384,512]{1,0:T(8,128)S(1)} custom-call(bf16[4,512,512]{2,1,0:T(8,128)(2,1)S(1)} %bitcast.6), custom_call_target="tpu_custom_call" | custom-call | flops 1073741824 | bytes 4194304 | tf_op jit(solution)/shard_map/pallas_call | solution.py:109
  71.3 0.1 collective-permute-start
  71.4 1.3 %shard_map.18 = (f32[384,512]{1,0:T(8,128)S(1)}, f32[512,512]{1,0:T(8,128)S(1)}) custom-call(bf16[4,512,512]{2,1,0:T(8,128)(2,1)S(1)} %bitcast.7), custom_call_target="tpu_custom_call" | custom-call | flops 1073741824 | bytes 4194304 | tf_op jit(solution)/shard_map/pallas_call | solution.py:109
  72.6 0.6 collective-permute-start.2
  73.2 0.4 collective-permute-done.other_ref
  73.6 6.5 %shard_map.20.own_ref = bf16[512,512]{1,0:T(8,128)(2,1)S(1)} custom-call(f32[384,512]{1,0:T(8,128)S(1)} %get-tuple-element.7.own_ref, f32[384,512]{1,0:T(8,128)S(1)} %collective-permute-done.other_ref), custom_call_target="tpu_custom_call" | custom-call | flops 5368709120 | bytes 2621440 | tf_op jit(solution)/shard_map/pallas_call | solution.py:150
  80.1 0.2 collective-permute-start.1
  80.3 0.0 collective-permute-done.2.other_ref
  80.3 0.1 shard_map.21.mean_ref
  80.4 1.7 %collective-permute-done.1.other_ref = bf16[512,512]{1,0:T(8,128)(2,1)S(1)} collective-permute-done((bf16[512,512]{1,0:T(8,128)(2,1)S(1)}, bf16[512,512]{1,0:T(8,128)(2,1)S(1)}, u32[]{:S(2)}, u32[]{:S(2)}) %collective-permute-start.1) | collective-permute-done | bytes 524320 | tf_op jit(solution)/shard_map/ppermute | solution.py:201
  82.1 0.7 shard_map.22
  82.9 17.1 %all_to_all.11 = bf16[32,16,256]{2,1,0:T(8,128)(2,1)S(1)} all-to-all(bf16[32,16,256]{2,1,0:T(8,128)(2,1)S(1)} %bitcast.8), channel_id=1, replica_groups=mesh['x'=4,'core'=2,'y'=4,'z'=8] {'y','z'}, dimensions={0} | all-to-all | bytes 524288 | tf_op jit(solution)/shard_map/all_to_all | solution.py:215
  99.9 0.8 copy.3
Async XLA Ops:
  71.3 2.4 %collective-permute-start = (f32[384,512]{1,0:T(8,128)S(1)}, f32[384,512]{1,0:T(8,128)S(1)}, u32[]{:S(2)}, u32[]{:S(2)}) collective-permute-start(f32[384,512]{1,0:T(8,128)S(1)} %shard_map.19), channel_id=1, source_target_pairs={{0,32},{32,0},{1,33},{33,1},{2,34},{34,2},{3,35},{35,3},{4,36},{36... | collective-permute-start | bytes 2359304 | tf_op jit(solution)/shard_map/ppermute | solution.py:201
  72.6 7.7 %collective-permute-start.2 = (f32[512,512]{1,0:T(8,128)S(1)}, f32[512,512]{1,0:T(8,128)S(1)}, u32[]{:S(2)}, u32[]{:S(2)}) collective-permute-start(f32[512,512]{1,0:T(8,128)S(1)} %get-tuple-element.8.own_ref), channel_id=1, source_target_pairs={{0,32},{32,0},{1,33},{33,1},{2,34},{34,2},{3,35},{35,3},{4,36},{36... | collective-permute-start | bytes 3145736 | tf_op jit(solution)/shard_map/ppermute | solution.py:201
  80.1 2.0 %collective-permute-start.1 = (bf16[512,512]{1,0:T(8,128)(2,1)S(1)}, bf16[512,512]{1,0:T(8,128)(2,1)S(1)}, u32[]{:S(2)}, u32[]{:S(2)}) collective-permute-start(bf16[512,512]{1,0:T(8,128)(2,1)S(1)} %shard_map.20.own_ref), channel_id=1, source_target_pairs={{0,32},{32,0},{1,33},{33,1},{2,34},{34,2},{3,35},{35,3},{4,36},{36... | collective-permute-start | bytes 1572872 | tf_op jit(solution)/shard_map/ppermute | solution.py:201

commit v6 on v5

--- a/solution.py
+++ b/solution.py
@@ -27,6 +27,16 @@
 
 def dot_tn(a, b):
     return lax.dot_general(a, b, (((0,), (0,)), ((), ())), preferred_element_type=jnp.float32)
+
+
+def split_product(a, b):
+    a_high, b_high = a.astype(jnp.bfloat16), b.astype(jnp.bfloat16)
+    a_low = (a - a_high.astype(jnp.float32)).astype(jnp.bfloat16)
+    b_low = (b - b_high.astype(jnp.float32)).astype(jnp.bfloat16)
+    return dot_nn(
+        jnp.concatenate([a_high, a_high, a_low], axis=1),
+        jnp.concatenate([b_high, b_low, b_high], axis=0),
+    )
 
 
 def relayout_kernel(in_ref, out_ref, landed, sems):
@@ -137,7 +147,8 @@
         hb = h.astype(jnp.bfloat16)
         if iteration + 2 < ITERS:
             y = f if y is None else y + f - dot_nn(y.astype(jnp.bfloat16), fb)
-            f = growth * (f - dot_nn(hb, fb))
+            hf = split_product(h, f) if iteration < 2 else dot_nn(hb, fb)
+            f = growth * (f - hf)
         else:
             af = f - f_squared
             w = f + growth * (af - dot_nn(hb, af.astype(jnp.bfloat16)))

time: 101 us -> 102 us (level)
    pallas_call x1, Pallas kernels: 6.47 us -> 7.53 us  [inverse_root(): pl.pallas_call(root_kernel, out_shape=jax.ShapeDtypeStruct((BLOCK, BLOCK)...]
  transfers between devices with their start and end apart: 3 -> 3, of which waited for: 2 -> 2; matrix products, arithmetic and copies ran while one was open for 0% -> 0% of each run, Pallas kernels for 8% -> 9%
where the time goes in v6:
time: 102 us
  blocking collectives  85.7 us (84%)
  Pallas kernels  12.2 us (12%)
  waiting for transfers between devices  1.91 us (2%)
  starting transfers between devices  1.09 us (1%)
    all_to_all x1, blocking collectives, per_device(): lax.all_to_all(send, ('x', 'y', 'z'), split_axis=0, concat_axis=0, tiled=...  68.6 us
    all_to_all x1, blocking collectives, per_device(): lax.all_to_all(piece.reshape(STRIPS, 16, HALF), ('y', 'z'), split_axis=0,...  17.1 us
    pallas_call x1, Pallas kernels, inverse_root(): pl.pallas_call(root_kernel, out_shape=jax.ShapeDtypeStruct((BLOCK, BLOCK)...  7.53 us
    pallas_call x2, Pallas kernels, gram(): pl.pallas_call(kernel, out_shape=[jax.ShapeDtypeStruct((n, BLOCK), jnp.fl...  2.27 us
  transfers between devices with their start and end apart: 3, of which 2 were waited for; matrix products, arithmetic and copies ran while one was open for 0% of the time, Pallas kernels for 9%

profile of v6, /device:TPU:32, one launch (start us, length us, event | category | flops | bytes accessed | tf_op | source)
XLA Modules:
  0.0 101.8 jit_solution(17061057818745752133)
XLA Ops:
  0.0 1.6 %shard_map.17 = bf16[128,16,512]{2,1,0:T(8,128)(2,1)S(1)} custom-call(bf16[16,65536]{1,0:T(8,128)(2,1)} %bitcast.9), custom_call_target="tpu_custom_call" | custom-call | tf_op jit(solution)/shard_map/pallas_call | solution.py:58
  1.6 68.6 %all_to_all.10 = bf16[128,16,512]{2,1,0:T(8,128)(2,1)S(1)} all-to-all(bf16[128,16,512]{2,1,0:T(8,128)(2,1)S(1)} %shard_map.17), channel_id=1, replica_groups=mesh['x'=4,'core'=2,'y'=4,'z'=8] {'x','y','z'}, dimensions={0} | all-to-all | bytes 4194304 | tf_op jit(solution)/shard_map/all_to_all | solution.py:217
  70.2 1.0 %shard_map.19 = f32[384,512]{1,0:T(8,128)S(1)} custom-call(bf16[4,512,512]{2,1,0:T(8,128)(2,1)S(1)} %bitcast.6), custom_call_target="tpu_custom_call" | custom-call | flops 1073741824 | bytes 4194304 | tf_op jit(solution)/shard_map/pallas_call | solution.py:119
  71.3 0.1 collective-permute-start
  71.4 1.3 %shard_map.18 = (f32[384,512]{1,0:T(8,128)S(1)}, f32[512,512]{1,0:T(8,128)S(1)}) custom-call(bf16[4,512,512]{2,1,0:T(8,128)(2,1)S(1)} %bitcast.7), custom_call_target="tpu_custom_call" | custom-call | flops 1073741824 | bytes 4194304 | tf_op jit(solution)/shard_map/pallas_call | solution.py:119
  72.6 0.8 collective-permute-start.2
  73.4 0.2 collective-permute-done.other_ref
  73.6 7.5 %shard_map.20.own_ref = bf16[512,512]{1,0:T(8,128)(2,1)S(1)} custom-call(f32[384,512]{1,0:T(8,128)S(1)} %get-tuple-element.7.own_ref, f32[384,512]{1,0:T(8,128)S(1)} %collective-permute-done.other_ref), custom_call_target="tpu_custom_call" | custom-call | flops 5368709120 | bytes 2621440 | tf_op jit(solution)/shard_map/pallas_call | solution.py:161
  81.2 0.2 collective-permute-start.1
  81.4 0.0 collective-permute-done.2.other_ref
  81.4 0.1 shard_map.21.mean_ref
  81.5 1.7 %collective-permute-done.1.other_ref = bf16[512,512]{1,0:T(8,128)(2,1)S(1)} collective-permute-done((bf16[512,512]{1,0:T(8,128)(2,1)S(1)}, bf16[512,512]{1,0:T(8,128)(2,1)S(1)}, u32[]{:S(2)}, u32[]{:S(2)}) %collective-permute-start.1) | collective-permute-done | bytes 524320 | tf_op jit(solution)/shard_map/ppermute | solution.py:212
  83.2 0.7 shard_map.22
  83.9 17.1 %all_to_all.11 = bf16[32,16,256]{2,1,0:T(8,128)(2,1)S(1)} all-to-all(bf16[32,16,256]{2,1,0:T(8,128)(2,1)S(1)} %bitcast.8), channel_id=1, replica_groups=mesh['x'=4,'core'=2,'y'=4,'z'=8] {'y','z'}, dimensions={0} | all-to-all | bytes 524288 | tf_op jit(solution)/shard_map/all_to_all | solution.py:226
  101.0 0.8 copy.3
Async XLA Ops:
  71.3 2.4 %collective-permute-start = (f32[384,512]{1,0:T(8,128)S(1)}, f32[384,512]{1,0:T(8,128)S(1)}, u32[]{:S(2)}, u32[]{:S(2)}) collective-permute-start(f32[384,512]{1,0:T(8,128)S(1)} %shard_map.19), channel_id=1, source_target_pairs={{0,32},{32,0},{1,33},{33,1},{2,34},{34,2},{3,35},{35,3},{4,36},{36... | collective-permute-start | bytes 2359304 | tf_op jit(solution)/shard_map/ppermute | solution.py:212
  72.6 8.8 %collective-permute-start.2 = (f32[512,512]{1,0:T(8,128)S(1)}, f32[512,512]{1,0:T(8,128)S(1)}, u32[]{:S(2)}, u32[]{:S(2)}) collective-permute-start(f32[512,512]{1,0:T(8,128)S(1)} %get-tuple-element.8.own_ref), channel_id=1, source_target_pairs={{0,32},{32,0},{1,33},{33,1},{2,34},{34,2},{3,35},{35,3},{4,36},{36... | collective-permute-start | bytes 3145736 | tf_op jit(solution)/shard_map/ppermute | solution.py:212
  81.2 2.0 %collective-permute-start.1 = (bf16[512,512]{1,0:T(8,128)(2,1)S(1)}, bf16[512,512]{1,0:T(8,128)(2,1)S(1)}, u32[]{:S(2)}, u32[]{:S(2)}) collective-permute-start(bf16[512,512]{1,0:T(8,128)(2,1)S(1)} %shard_map.20.own_ref), channel_id=1, source_target_pairs={{0,32},{32,0},{1,33},{33,1},{2,34},{34,2},{3,35},{35,3},{4,36},{36... | collective-permute-start | bytes 1572872 | tf_op jit(solution)/shard_map/ppermute | solution.py:212

commit v7 on v6

--- a/solution.py
+++ b/solution.py
@@ -127,14 +127,16 @@
 
 
 def root_kernel(own_ref, other_ref, out_ref):
-    row = lax.broadcasted_iota(jnp.int32, (BLOCK, BLOCK), 0)
-    col = lax.broadcasted_iota(jnp.int32, (BLOCK, BLOCK), 1)
+    row = lax.broadcasted_iota(jnp.int32, (QUARTER, QUARTER), 0)
+    col = lax.broadcasted_iota(jnp.int32, (QUARTER, QUARTER), 1)
     diagonal = row == col
+    tiles = [slice(start, start + QUARTER) for start in range(0, BLOCK, QUARTER)]
     packed = own_ref[...] + other_ref[...]
     low = jnp.concatenate([packed[HALF:, :HALF], packed[HALF:, HALF:]], axis=0)
     low = jnp.concatenate([packed[:HALF, HALF:].T, low], axis=1)
     stat = jnp.concatenate([packed[:HALF], low], axis=0)
-    trace = jnp.sum(jnp.where(diagonal, stat, 0.0), keepdims=True)
+    on_diagonal = sum(jnp.where(diagonal, stat[tile, tile], 0.0) for tile in tiles)
+    trace = jnp.sum(on_diagonal, keepdims=True)
     growth = 1.25**4
     f = stat * (0.2 / trace)
     y = None
@@ -147,14 +149,17 @@
         hb = h.astype(jnp.bfloat16)
         if iteration + 2 < ITERS:
             y = f if y is None else y + f - dot_nn(y.astype(jnp.bfloat16), fb)
-            hf = split_product(h, f) if iteration < 2 else dot_nn(hb, fb)
+            hf = split_product(h, f) if iteration == 0 else dot_nn(hb, fb)
             f = growth * (f - hf)
         else:
             af = f - f_squared
             w = f + growth * (af - dot_nn(hb, af.astype(jnp.bfloat16)))
             y = y + w - dot_nn(y.astype(jnp.bfloat16), w.astype(jnp.bfloat16))
     scale = lax.rsqrt(jnp.sqrt(trace * (1.0 / (GROUPS * BLOCK)))) * 1.25**ITERS
-    out_ref[...] = (scale * (jnp.where(diagonal, 1.0, 0.0) - y)).astype(jnp.bfloat16)
+    out_ref[...] = (-scale * y).astype(jnp.bfloat16)
+    for tile in tiles:
+        x = scale * (jnp.where(diagonal, 1.0, 0.0) - y[tile, tile])
+        out_ref[tile, tile] = x.astype(jnp.bfloat16)
 
 
 def inverse_root(own, other):

time: 102 us -> 101 us (level)
  transfers between devices with their start and end apart: 3 -> 3, of which waited for: 2 -> 2; matrix products, arithmetic and copies ran while one was open for 0% -> 0% of each run, Pallas kernels for 9% -> 8%
where the time goes in v7:
time: 101 us
  blocking collectives  85.7 us (85%)
  Pallas kernels  11.5 us (11%)
  waiting for transfers between devices  2.1 us (2%)
    all_to_all x1, blocking collectives, per_device(): lax.all_to_all(send, ('x', 'y', 'z'), split_axis=0, concat_axis=0, tiled=...  68.6 us
    all_to_all x1, blocking collectives, per_device(): lax.all_to_all(piece.reshape(STRIPS, 16, HALF), ('y', 'z'), split_axis=0,...  17 us
    pallas_call x1, Pallas kernels, inverse_root(): pl.pallas_call(root_kernel, out_shape=jax.ShapeDtypeStruct((BLOCK, BLOCK)...  6.83 us
    pallas_call x2, Pallas kernels, gram(): pl.pallas_call(kernel, out_shape=[jax.ShapeDtypeStruct((n, BLOCK), jnp.fl...  2.28 us
    ppermute x3, waiting for transfers between devices, swap_cores(): return lax.ppermute(x, 'core', [(0, 1), (1, 0)])  2.1 us
  transfers between devices with their start and end apart: 3, of which 2 were waited for; matrix products, arithmetic and copies ran while one was open for 0% of the time, Pallas kernels for 8%

profile of v7, /device:TPU:32, one launch (start us, length us, event | category | flops | bytes accessed | tf_op | source)
XLA Modules:
  0.0 101.0 jit_solution(9206676852542335813)
XLA Ops:
  0.0 1.6 %shard_map.17 = bf16[128,16,512]{2,1,0:T(8,128)(2,1)S(1)} custom-call(bf16[16,65536]{1,0:T(8,128)(2,1)} %bitcast.9), custom_call_target="tpu_custom_call" | custom-call | tf_op jit(solution)/shard_map/pallas_call | solution.py:58
  1.6 68.6 %all_to_all.10 = bf16[128,16,512]{2,1,0:T(8,128)(2,1)S(1)} all-to-all(bf16[128,16,512]{2,1,0:T(8,128)(2,1)S(1)} %shard_map.17), channel_id=1, replica_groups=mesh['x'=4,'core'=2,'y'=4,'z'=8] {'x','y','z'}, dimensions={0} | all-to-all | bytes 4194304 | tf_op jit(solution)/shard_map/all_to_all | solution.py:222
  70.2 1.0 %shard_map.19 = f32[384,512]{1,0:T(8,128)S(1)} custom-call(bf16[4,512,512]{2,1,0:T(8,128)(2,1)S(1)} %bitcast.6), custom_call_target="tpu_custom_call" | custom-call | flops 1073741824 | bytes 4194304 | tf_op jit(solution)/shard_map/pallas_call | solution.py:119
  71.3 0.1 collective-permute-start
  71.4 1.3 %shard_map.18 = (f32[384,512]{1,0:T(8,128)S(1)}, f32[512,512]{1,0:T(8,128)S(1)}) custom-call(bf16[4,512,512]{2,1,0:T(8,128)(2,1)S(1)} %bitcast.7), custom_call_target="tpu_custom_call" | custom-call | flops 1073741824 | bytes 4194304 | tf_op jit(solution)/shard_map/pallas_call | solution.py:119
  72.6 0.6 collective-permute-start.2
  73.2 0.4 collective-permute-done.other_ref
  73.6 6.8 %shard_map.20.own_ref = bf16[512,512]{1,0:T(8,128)(2,1)S(1)} custom-call(f32[384,512]{1,0:T(8,128)S(1)} %get-tuple-element.7.own_ref, f32[384,512]{1,0:T(8,128)S(1)} %collective-permute-done.other_ref), custom_call_target="tpu_custom_call" | custom-call | flops 5368709120 | bytes 2621440 | tf_op jit(solution)/shard_map/pallas_call | solution.py:166
  80.5 0.2 collective-permute-start.1
  80.7 0.0 collective-permute-done.2.other_ref
  80.7 0.1 shard_map.21.mean_ref
  80.8 1.7 %collective-permute-done.1.other_ref = bf16[512,512]{1,0:T(8,128)(2,1)S(1)} collective-permute-done((bf16[512,512]{1,0:T(8,128)(2,1)S(1)}, bf16[512,512]{1,0:T(8,128)(2,1)S(1)}, u32[]{:S(2)}, u32[]{:S(2)}) %collective-permute-start.1) | collective-permute-done | bytes 524320 | tf_op jit(solution)/shard_map/ppermute | solution.py:217
  82.5 0.7 shard_map.22
  83.2 17.0 %all_to_all.11 = bf16[32,16,256]{2,1,0:T(8,128)(2,1)S(1)} all-to-all(bf16[32,16,256]{2,1,0:T(8,128)(2,1)S(1)} %bitcast.8), channel_id=1, replica_groups=mesh['x'=4,'core'=2,'y'=4,'z'=8] {'y','z'}, dimensions={0} | all-to-all | bytes 524288 | tf_op jit(solution)/shard_map/all_to_all | solution.py:231
  100.3 0.8 copy.3
Async XLA Ops:
  71.3 2.4 %collective-permute-start = (f32[384,512]{1,0:T(8,128)S(1)}, f32[384,512]{1,0:T(8,128)S(1)}, u32[]{:S(2)}, u32[]{:S(2)}) collective-permute-start(f32[384,512]{1,0:T(8,128)S(1)} %shard_map.19), channel_id=1, source_target_pairs={{0,32},{32,0},{1,33},{33,1},{2,34},{34,2},{3,35},{35,3},{4,36},{36... | collective-permute-start | bytes 2359304 | tf_op jit(solution)/shard_map/ppermute | solution.py:217
  72.6 8.1 %collective-permute-start.2 = (f32[512,512]{1,0:T(8,128)S(1)}, f32[512,512]{1,0:T(8,128)S(1)}, u32[]{:S(2)}, u32[]{:S(2)}) collective-permute-start(f32[512,512]{1,0:T(8,128)S(1)} %get-tuple-element.8.own_ref), channel_id=1, source_target_pairs={{0,32},{32,0},{1,33},{33,1},{2,34},{34,2},{3,35},{35,3},{4,36},{36... | collective-permute-start | bytes 3145736 | tf_op jit(solution)/shard_map/ppermute | solution.py:217
  80.5 2.0 %collective-permute-start.1 = (bf16[512,512]{1,0:T(8,128)(2,1)S(1)}, bf16[512,512]{1,0:T(8,128)(2,1)S(1)}, u32[]{:S(2)}, u32[]{:S(2)}) collective-permute-start(bf16[512,512]{1,0:T(8,128)(2,1)S(1)} %shard_map.20.own_ref), channel_id=1, source_target_pairs={{0,32},{32,0},{1,33},{33,1},{2,34},{34,2},{3,35},{35,3},{4,36},{36... | collective-permute-start | bytes 1572872 | tf_op jit(solution)/shard_map/ppermute | solution.py:217

commit v8 on v7

--- a/solution.py
+++ b/solution.py
@@ -50,8 +50,7 @@
     for chunk in range(CHUNKS):
         copies[chunk].wait()
         for index in range(chunk * CHUNK // BLOCK, (chunk + 1) * CHUNK // BLOCK):
-            strip, k = divmod(index, PER_STRIP)
-            out_ref[k * STRIPS + strip] = landed[:, index * BLOCK : (index + 1) * BLOCK]
+            out_ref[index] = landed[:, index * BLOCK : (index + 1) * BLOCK]
 
 
 def relayout(rows):
@@ -68,8 +67,12 @@
     )(rows)
 
 
+def group_block(in_ref, group):
+    return in_ref[:, group].reshape(BLOCK, BLOCK)
+
+
 def left_gram(in_ref, out_ref):
-    wide = jnp.concatenate([in_ref[g] for g in range(PER_STRIP)], axis=1)
+    wide = jnp.concatenate([group_block(in_ref, g) for g in range(PER_STRIP)], axis=1)
     low = wide[HALF:]
     store_gram(dot_nt(wide[:HALF], wide), dot_nt(low, low), out_ref)
 
@@ -109,9 +112,9 @@
     def _():
         right_gram(in_ref, keep_ref)
 
-    total = in_ref[0].astype(jnp.float32)
+    total = group_block(in_ref, 0).astype(jnp.float32)
     for group in range(1, PER_STRIP):
-        total += in_ref[group].astype(jnp.float32)
+        total += group_block(in_ref, group).astype(jnp.float32)
     mean_ref[...] = total
 
 
@@ -219,8 +222,8 @@
 
 def per_device(gradients):
     send = relayout(gradients[0])
-    arrived = lax.all_to_all(send, ("x", "y", "z"), split_axis=0, concat_axis=0, tiled=True)
-    blocks = arrived.reshape(PER_STRIP, BLOCK, BLOCK)
+    arrived = lax.all_to_all(send, ("y", "z", "x"), split_axis=0, concat_axis=0, tiled=True)
+    blocks = arrived.reshape(STRIPS, PER_STRIP, 16, BLOCK)
     (other,) = gram(send_kernel, (HALF + QUARTER,), blocks)
     stat_other = swap_cores(other)
     keep, mean_own = gram(keep_kernel, (HALF + QUARTER, BLOCK), blocks)

time: 101 us -> 100 us (0.990)
  blocking collectives: 85.7 us -> 84.6 us
    all_to_all x1, blocking collectives: 68.6 us -> 67.1 us  [per_device(): lax.all_to_all(send, ('y', 'z', 'x'), split_axis=0, concat_axis=0, tiled=...]
where the time goes in v8:
time: 100 us
  blocking collectives  84.6 us (85%)
  Pallas kernels  11.5 us (12%)
  waiting for transfers between devices  2.1 us (2%)
    all_to_all x1, blocking collectives, per_device(): lax.all_to_all(send, ('y', 'z', 'x'), split_axis=0, concat_axis=0, tiled=...  67.1 us
    all_to_all x1, blocking collectives, per_device(): lax.all_to_all(piece.reshape(STRIPS, 16, HALF), ('y', 'z'), split_axis=0,...  17.5 us
    pallas_call x1, Pallas kernels, inverse_root(): pl.pallas_call(root_kernel, out_shape=jax.ShapeDtypeStruct((BLOCK, BLOCK)...  6.83 us
    pallas_call x2, Pallas kernels, gram(): pl.pallas_call(kernel, out_shape=[jax.ShapeDtypeStruct((n, BLOCK), jnp.fl...  2.28 us
    ppermute x3, waiting for transfers between devices, swap_cores(): return lax.ppermute(x, 'core', [(0, 1), (1, 0)])  2.1 us
  transfers between devices with their start and end apart: 3, of which 2 were waited for; matrix products, arithmetic and copies ran while one was open for 0% of the time, Pallas kernels for 8%

profile of v8, /device:TPU:32, one launch (start us, length us, event | category | flops | bytes accessed | tf_op | source)
XLA Modules:
  0.0 100.0 jit_solution(10169028873132918956)
XLA Ops:
  0.0 1.6 %shard_map.17 = bf16[128,16,512]{2,1,0:T(8,128)(2,1)S(1)} custom-call(bf16[16,65536]{1,0:T(8,128)(2,1)} %bitcast.9), custom_call_target="tpu_custom_call" | custom-call | tf_op jit(solution)/shard_map/pallas_call | solution.py:57
  1.6 67.1 %all_to_all.10 = bf16[128,16,512]{2,1,0:T(8,128)(2,1)S(1)} all-to-all(bf16[128,16,512]{2,1,0:T(8,128)(2,1)S(1)} %shard_map.17), channel_id=1, replica_groups=mesh['x'=4,'core'=2,'y'=4,'z'=8] {'y','z','x'}, dimensions={0} | all-to-all | bytes 4194304 | tf_op jit(solution)/shard_map/all_to_all | solution.py:225
  68.7 1.0 %shard_map.19 = f32[384,512]{1,0:T(8,128)S(1)} custom-call(bf16[32,4,16,512]{3,2,1,0:T(8,128)(2,1)S(1)} %bitcast.6), custom_call_target="tpu_custom_call" | custom-call | flops 1073741824 | bytes 4194304 | tf_op jit(solution)/shard_map/pallas_call | solution.py:122
  69.7 0.1 collective-permute-start
  69.8 1.3 %shard_map.18 = (f32[384,512]{1,0:T(8,128)S(1)}, f32[512,512]{1,0:T(8,128)S(1)}) custom-call(bf16[32,4,16,512]{3,2,1,0:T(8,128)(2,1)S(1)} %bitcast.7), custom_call_target="tpu_custom_call" | custom-call | flops 1073741824 | bytes 4194304 | tf_op jit(solution)/shard_map/pallas_call | solution.py:122
  71.1 0.6 collective-permute-start.2
  71.7 0.4 collective-permute-done.other_ref
  72.1 6.8 %shard_map.20.own_ref = bf16[512,512]{1,0:T(8,128)(2,1)S(1)} custom-call(f32[384,512]{1,0:T(8,128)S(1)} %get-tuple-element.7.own_ref, f32[384,512]{1,0:T(8,128)S(1)} %collective-permute-done.other_ref), custom_call_target="tpu_custom_call" | custom-call | flops 5368709120 | bytes 2621440 | tf_op jit(solution)/shard_map/pallas_call | solution.py:169
  78.9 0.2 collective-permute-start.1
  79.1 0.0 collective-permute-done.2.other_ref
  79.1 0.1 shard_map.21.mean_ref
  79.2 1.7 %collective-permute-done.1.other_ref = bf16[512,512]{1,0:T(8,128)(2,1)S(1)} collective-permute-done((bf16[512,512]{1,0:T(8,128)(2,1)S(1)}, bf16[512,512]{1,0:T(8,128)(2,1)S(1)}, u32[]{:S(2)}, u32[]{:S(2)}) %collective-permute-start.1) | collective-permute-done | bytes 524320 | tf_op jit(solution)/shard_map/ppermute | solution.py:220
  80.9 0.7 shard_map.22
  81.7 17.5 %all_to_all.11 = bf16[32,16,256]{2,1,0:T(8,128)(2,1)S(1)} all-to-all(bf16[32,16,256]{2,1,0:T(8,128)(2,1)S(1)} %bitcast.8), channel_id=1, replica_groups=mesh['x'=4,'core'=2,'y'=4,'z'=8] {'y','z'}, dimensions={0} | all-to-all | bytes 524288 | tf_op jit(solution)/shard_map/all_to_all | solution.py:234
  99.2 0.8 copy.3
Async XLA Ops:
  69.7 2.4 %collective-permute-start = (f32[384,512]{1,0:T(8,128)S(1)}, f32[384,512]{1,0:T(8,128)S(1)}, u32[]{:S(2)}, u32[]{:S(2)}) collective-permute-start(f32[384,512]{1,0:T(8,128)S(1)} %shard_map.19), channel_id=1, source_target_pairs={{0,32},{32,0},{1,33},{33,1},{2,34},{34,2},{3,35},{35,3},{4,36},{36... | collective-permute-start | bytes 2359304 | tf_op jit(solution)/shard_map/ppermute | solution.py:220
  71.1 8.1 %collective-permute-start.2 = (f32[512,512]{1,0:T(8,128)S(1)}, f32[512,512]{1,0:T(8,128)S(1)}, u32[]{:S(2)}, u32[]{:S(2)}) collective-permute-start(f32[512,512]{1,0:T(8,128)S(1)} %get-tuple-element.8.own_ref), channel_id=1, source_target_pairs={{0,32},{32,0},{1,33},{33,1},{2,34},{34,2},{3,35},{35,3},{4,36},{36... | collective-permute-start | bytes 3145736 | tf_op jit(solution)/shard_map/ppermute | solution.py:220
  78.9 2.0 %collective-permute-start.1 = (bf16[512,512]{1,0:T(8,128)(2,1)S(1)}, bf16[512,512]{1,0:T(8,128)(2,1)S(1)}, u32[]{:S(2)}, u32[]{:S(2)}) collective-permute-start(bf16[512,512]{1,0:T(8,128)(2,1)S(1)} %shard_map.20.own_ref), channel_id=1, source_target_pairs={{0,32},{32,0},{1,33},{33,1},{2,34},{34,2},{3,35},{35,3},{4,36},{36... | collective-permute-start | bytes 1572872 | tf_op jit(solution)/shard_map/ppermute | solution.py:220

commit v9 on v8

--- a/solution.py
+++ b/solution.py
@@ -13,6 +13,7 @@
 STRIPS = 32
 HALF = 256
 QUARTER = 128
+DEPTH = 8
 CHUNKS = 8
 CHUNK = 8192
 
@@ -197,7 +198,11 @@
     def piece(left_ref, right_ref, start):
         right = right_ref[:, start : start + HALF]
         inner = dot_nn(mean_ref[...], right).astype(jnp.bfloat16)
-        out_ref[...] = dot_nn(left_ref[...], inner).astype(jnp.bfloat16)
+        update = dot_nn(left_ref[...], inner).astype(jnp.bfloat16)
+        update = update.reshape(STRIPS, 16, HALF)
+        for y in range(STRIPS // DEPTH):
+            for z in range(DEPTH):
+                out_ref[z, y] = update[y * DEPTH + z]
 
     @pl.when(side == 0)
     def _():
@@ -211,7 +216,7 @@
 def update_piece(own, other, mean):
     return pl.pallas_call(
         update_kernel,
-        out_shape=jax.ShapeDtypeStruct((BLOCK, HALF), jnp.bfloat16),
+        out_shape=jax.ShapeDtypeStruct((DEPTH, STRIPS // DEPTH, 16, HALF), jnp.bfloat16),
         compiler_params=pltpu.CompilerParams(vmem_limit_bytes=32 * 1024 * 1024),
     )(own, other, mean)
 
@@ -232,9 +237,10 @@
     other_root = swap_cores(own_root)
     piece = update_piece(own_root, other_root, mean_block(mean_own, mean_other))
     rows = lax.all_to_all(
-        piece.reshape(STRIPS, 16, HALF), ("y", "z"), split_axis=0, concat_axis=0, tiled=True
+        piece.reshape(STRIPS, 16, HALF), ("z", "y"), split_axis=0, concat_axis=0, tiled=True
     )
-    return jnp.swapaxes(rows, 0, 1)[:, :, None, :]
+    rows = rows.reshape(DEPTH, STRIPS // DEPTH, 16, HALF).transpose(2, 1, 0, 3)
+    return rows.reshape(16, STRIPS, 1, HALF)
 
 
 def solution(mesh):

time: 100 us -> 100 us (level)
  no operation moved by 1% of the time
where the time goes in v9:
time: 100 us; the launch traced here: 99.9 us
  blocking collectives  84.5 us (84%)
  Pallas kernels  11.5 us (12%)
  waiting for transfers between devices  2.1 us (2%)
    all_to_all x1, blocking collectives, per_device(): lax.all_to_all(send, ('y', 'z', 'x'), split_axis=0, concat_axis=0, tiled=...  67.1 us
    all_to_all x1, blocking collectives, per_device(): lax.all_to_all(piece.reshape(STRIPS, 16, HALF), ('z', 'y'), split_axis=0,...  17.4 us
    pallas_call x1, Pallas kernels, inverse_root(): pl.pallas_call(root_kernel, out_shape=jax.ShapeDtypeStruct((BLOCK, BLOCK)...  6.83 us
    pallas_call x2, Pallas kernels, gram(): pl.pallas_call(kernel, out_shape=[jax.ShapeDtypeStruct((n, BLOCK), jnp.fl...  2.28 us
    ppermute x3, waiting for transfers between devices, swap_cores(): return lax.ppermute(x, 'core', [(0, 1), (1, 0)])  2.1 us
  transfers between devices with their start and end apart: 3, of which 2 were waited for; matrix products, arithmetic and copies ran while one was open for 0% of the time, Pallas kernels for 8%

profile of v9, /device:TPU:32, one launch (start us, length us, event | category | flops | bytes accessed | tf_op | source)
XLA Modules:
  0.0 99.9 jit_solution(6135858312021074399)
XLA Ops:
  0.0 1.6 %shard_map.17 = bf16[128,16,512]{2,1,0:T(8,128)(2,1)S(1)} custom-call(bf16[16,65536]{1,0:T(8,128)(2,1)} %bitcast.12), custom_call_target="tpu_custom_call" | custom-call | tf_op jit(solution)/shard_map/pallas_call | solution.py:58
  1.6 67.1 %all_to_all.10 = bf16[128,16,512]{2,1,0:T(8,128)(2,1)S(1)} all-to-all(bf16[128,16,512]{2,1,0:T(8,128)(2,1)S(1)} %shard_map.17), channel_id=1, replica_groups=mesh['x'=4,'core'=2,'y'=4,'z'=8] {'y','z','x'}, dimensions={0} | all-to-all | bytes 4194304 | tf_op jit(solution)/shard_map/all_to_all | solution.py:230
  68.7 1.0 %shard_map.19 = f32[384,512]{1,0:T(8,128)S(1)} custom-call(bf16[32,4,16,512]{3,2,1,0:T(8,128)(2,1)S(1)} %bitcast.9), custom_call_target="tpu_custom_call" | custom-call | flops 1073741824 | bytes 4194304 | tf_op jit(solution)/shard_map/pallas_call | solution.py:123
  69.7 0.1 collective-permute-start
  69.8 1.3 %shard_map.18 = (f32[384,512]{1,0:T(8,128)S(1)}, f32[512,512]{1,0:T(8,128)S(1)}) custom-call(bf16[32,4,16,512]{3,2,1,0:T(8,128)(2,1)S(1)} %bitcast.10), custom_call_target="tpu_custom_call" | custom-call | flops 1073741824 | bytes 4194304 | tf_op jit(solution)/shard_map/pallas_call | solution.py:123
  71.1 0.6 collective-permute-start.2
  71.7 0.4 collective-permute-done.other_ref
  72.1 6.8 %shard_map.20.own_ref = bf16[512,512]{1,0:T(8,128)(2,1)S(1)} custom-call(f32[384,512]{1,0:T(8,128)S(1)} %get-tuple-element.7.own_ref, f32[384,512]{1,0:T(8,128)S(1)} %collective-permute-done.other_ref), custom_call_target="tpu_custom_call" | custom-call | flops 5368709120 | bytes 2621440 | tf_op jit(solution)/shard_map/pallas_call | solution.py:170
  78.9 0.2 collective-permute-start.1
  79.1 0.0 collective-permute-done.2.other_ref
  79.1 0.1 shard_map.21.mean_ref
  79.2 1.7 %collective-permute-done.1.other_ref = bf16[512,512]{1,0:T(8,128)(2,1)S(1)} collective-permute-done((bf16[512,512]{1,0:T(8,128)(2,1)S(1)}, bf16[512,512]{1,0:T(8,128)(2,1)S(1)}, u32[]{:S(2)}, u32[]{:S(2)}) %collective-permute-start.1) | collective-permute-done | bytes 524320 | tf_op jit(solution)/shard_map/ppermute | solution.py:225
  80.9 0.7 shard_map.22
  81.7 17.4 %all_to_all.11 = bf16[32,16,256]{2,1,0:T(8,128)(2,1)S(1)} all-to-all(bf16[32,16,256]{2,1,0:T(8,128)(2,1)S(1)} %bitcast.11), channel_id=1, replica_groups=mesh['x'=4,'core'=2,'y'=4,'z'=8] {'z','y'}, dimensions={0} | all-to-all | bytes 524288 | tf_op jit(solution)/shard_map/all_to_all | solution.py:239
  99.1 0.9 copy.4
Async XLA Ops:
  69.7 2.4 %collective-permute-start = (f32[384,512]{1,0:T(8,128)S(1)}, f32[384,512]{1,0:T(8,128)S(1)}, u32[]{:S(2)}, u32[]{:S(2)}) collective-permute-start(f32[384,512]{1,0:T(8,128)S(1)} %shard_map.19), channel_id=1, source_target_pairs={{0,32},{32,0},{1,33},{33,1},{2,34},{34,2},{3,35},{35,3},{4,36},{36... | collective-permute-start | bytes 2359304 | tf_op jit(solution)/shard_map/ppermute | solution.py:225
  71.1 8.1 %collective-permute-start.2 = (f32[512,512]{1,0:T(8,128)S(1)}, f32[512,512]{1,0:T(8,128)S(1)}, u32[]{:S(2)}, u32[]{:S(2)}) collective-permute-start(f32[512,512]{1,0:T(8,128)S(1)} %get-tuple-element.8.own_ref), channel_id=1, source_target_pairs={{0,32},{32,0},{1,33},{33,1},{2,34},{34,2},{3,35},{35,3},{4,36},{36... | collective-permute-start | bytes 3145736 | tf_op jit(solution)/shard_map/ppermute | solution.py:225
  78.9 2.0 %collective-permute-start.1 = (bf16[512,512]{1,0:T(8,128)(2,1)S(1)}, bf16[512,512]{1,0:T(8,128)(2,1)S(1)}, u32[]{:S(2)}, u32[]{:S(2)}) collective-permute-start(bf16[512,512]{1,0:T(8,128)(2,1)S(1)} %shard_map.20.own_ref), channel_id=1, source_target_pairs={{0,32},{32,0},{1,33},{33,1},{2,34},{34,2},{3,35},{35,3},{4,36},{36... | collective-permute-start | bytes 1572872 | tf_op jit(solution)/shard_map/ppermute | solution.py:225

commit v10 on v8

--- a/solution.py
+++ b/solution.py
@@ -129,6 +129,14 @@
     )(blocks)
 
 
+def halves(matrix):
+    return [matrix[:HALF], matrix[HALF:]]
+
+
+def as_bf16(parts):
+    return jnp.concatenate([part.astype(jnp.bfloat16) for part in parts])
+
+
 def root_kernel(own_ref, other_ref, out_ref):
     row = lax.broadcasted_iota(jnp.int32, (QUARTER, QUARTER), 0)
     col = lax.broadcasted_iota(jnp.int32, (QUARTER, QUARTER), 1)
@@ -141,23 +149,32 @@
     on_diagonal = sum(jnp.where(diagonal, stat[tile, tile], 0.0) for tile in tiles)
     trace = jnp.sum(on_diagonal, keepdims=True)
     growth = 1.25**4
-    f = stat * (0.2 / trace)
+    f = halves(stat * (0.2 / trace))
     y = None
     for iteration in range(ITERS - 1):
-        fb = f.astype(jnp.bfloat16)
-        f_squared = dot_nn(fb, fb)
-        g = 2.0 * f - f_squared
-        gb = g.astype(jnp.bfloat16)
-        h = 2.0 * g - dot_nn(gb, gb)
-        hb = h.astype(jnp.bfloat16)
+        fb = as_bf16(f)
+        f_squared = [dot_nn(part.astype(jnp.bfloat16), fb) for part in f]
+        g = [2.0 * part - square for part, square in zip(f, f_squared)]
+        gb = as_bf16(g)
+        h = [2.0 * part - dot_nn(part.astype(jnp.bfloat16), gb) for part in g]
         if iteration + 2 < ITERS:
-            y = f if y is None else y + f - dot_nn(y.astype(jnp.bfloat16), fb)
-            hf = split_product(h, f) if iteration == 0 else dot_nn(hb, fb)
-            f = growth * (f - hf)
+            if iteration == 0:
+                hf = halves(split_product(jnp.concatenate(h), jnp.concatenate(f)))
+            else:
+                hf = [dot_nn(part.astype(jnp.bfloat16), fb) for part in h]
+            if y is None:
+                y = f
+            else:
+                y = [p + q - dot_nn(p.astype(jnp.bfloat16), fb) for p, q in zip(y, f)]
+            f = [growth * (part - product) for part, product in zip(f, hf)]
         else:
-            af = f - f_squared
-            w = f + growth * (af - dot_nn(hb, af.astype(jnp.bfloat16)))
-            y = y + w - dot_nn(y.astype(jnp.bfloat16), w.astype(jnp.bfloat16))
+            af = [part - square for part, square in zip(f, f_squared)]
+            afb = as_bf16(af)
+            haf = [dot_nn(part.astype(jnp.bfloat16), afb) for part in h]
+            w = [p + growth * (q - product) for p, q, product in zip(f, af, haf)]
+            wb = as_bf16(w)
+            y = [p + q - dot_nn(p.astype(jnp.bfloat16), wb) for p, q in zip(y, w)]
+    y = jnp.concatenate(y)
     scale = lax.rsqrt(jnp.sqrt(trace * (1.0 / (GROUPS * BLOCK)))) * 1.25**ITERS
     out_ref[...] = (-scale * y).astype(jnp.bfloat16)
     for tile in tiles:

time: 100 us -> 100 us (level)
  no operation moved by 1% of the time
where the time goes in v10:
time: 100 us
  blocking collectives  84.6 us (85%)
  Pallas kernels  11.5 us (12%)
  waiting for transfers between devices  1.91 us (2%)
  starting transfers between devices  1.09 us (1%)
    all_to_all x1, blocking collectives, per_device(): lax.all_to_all(send, ('y', 'z', 'x'), split_axis=0, concat_axis=0, tiled=...  67.1 us
    all_to_all x1, blocking collectives, per_device(): lax.all_to_all(piece.reshape(STRIPS, 16, HALF), ('y', 'z'), split_axis=0,...  17.5 us
    pallas_call x1, Pallas kernels, inverse_root(): pl.pallas_call(root_kernel, out_shape=jax.ShapeDtypeStruct((BLOCK, BLOCK)...  6.83 us
    pallas_call x2, Pallas kernels, gram(): pl.pallas_call(kernel, out_shape=[jax.ShapeDtypeStruct((n, BLOCK), jnp.fl...  2.28 us
  transfers between devices with their start and end apart: 3, of which 2 were waited for; matrix products, arithmetic and copies ran while one was open for 0% of the time, Pallas kernels for 8%

profile of v10, /device:TPU:32, one launch (start us, length us, event | category | flops | bytes accessed | tf_op | source)
XLA Modules:
  0.0 100.0 jit_solution(3830832926888070328)
XLA Ops:
  0.0 1.6 %shard_map.17 = bf16[128,16,512]{2,1,0:T(8,128)(2,1)S(1)} custom-call(bf16[16,65536]{1,0:T(8,128)(2,1)} %bitcast.9), custom_call_target="tpu_custom_call" | custom-call | tf_op jit(solution)/shard_map/pallas_call | solution.py:57
  1.6 67.1 %all_to_all.10 = bf16[128,16,512]{2,1,0:T(8,128)(2,1)S(1)} all-to-all(bf16[128,16,512]{2,1,0:T(8,128)(2,1)S(1)} %shard_map.17), channel_id=1, replica_groups=mesh['x'=4,'core'=2,'y'=4,'z'=8] {'y','z','x'}, dimensions={0} | all-to-all | bytes 4194304 | tf_op jit(solution)/shard_map/all_to_all | solution.py:242
  68.7 1.0 %shard_map.19 = f32[384,512]{1,0:T(8,128)S(1)} custom-call(bf16[32,4,16,512]{3,2,1,0:T(8,128)(2,1)S(1)} %bitcast.6), custom_call_target="tpu_custom_call" | custom-call | flops 1073741824 | bytes 4194304 | tf_op jit(solution)/shard_map/pallas_call | solution.py:122
  69.7 0.1 collective-permute-start
  69.8 1.3 %shard_map.18 = (f32[384,512]{1,0:T(8,128)S(1)}, f32[512,512]{1,0:T(8,128)S(1)}) custom-call(bf16[32,4,16,512]{3,2,1,0:T(8,128)(2,1)S(1)} %bitcast.7), custom_call_target="tpu_custom_call" | custom-call | flops 1073741824 | bytes 4194304 | tf_op jit(solution)/shard_map/pallas_call | solution.py:122
  71.1 0.8 collective-permute-start.2
  71.8 0.2 collective-permute-done.other_ref
  72.1 6.8 %shard_map.20.own_ref = bf16[512,512]{1,0:T(8,128)(2,1)S(1)} custom-call(f32[384,512]{1,0:T(8,128)S(1)} %get-tuple-element.7.own_ref, f32[384,512]{1,0:T(8,128)S(1)} %collective-permute-done.other_ref), custom_call_target="tpu_custom_call" | custom-call | flops 5368709120 | bytes 2621440 | tf_op jit(solution)/shard_map/pallas_call | solution.py:186
  78.9 0.2 collective-permute-start.1
  79.2 0.0 collective-permute-done.2.other_ref
  79.2 0.1 shard_map.21.mean_ref
  79.3 1.7 %collective-permute-done.1.other_ref = bf16[512,512]{1,0:T(8,128)(2,1)S(1)} collective-permute-done((bf16[512,512]{1,0:T(8,128)(2,1)S(1)}, bf16[512,512]{1,0:T(8,128)(2,1)S(1)}, u32[]{:S(2)}, u32[]{:S(2)}) %collective-permute-start.1) | collective-permute-done | bytes 524320 | tf_op jit(solution)/shard_map/ppermute | solution.py:237
  80.9 0.7 shard_map.22
  81.7 17.5 %all_to_all.11 = bf16[32,16,256]{2,1,0:T(8,128)(2,1)S(1)} all-to-all(bf16[32,16,256]{2,1,0:T(8,128)(2,1)S(1)} %bitcast.8), channel_id=1, replica_groups=mesh['x'=4,'core'=2,'y'=4,'z'=8] {'y','z'}, dimensions={0} | all-to-all | bytes 524288 | tf_op jit(solution)/shard_map/all_to_all | solution.py:251
  99.2 0.8 copy.3
Async XLA Ops:
  69.7 2.4 %collective-permute-start = (f32[384,512]{1,0:T(8,128)S(1)}, f32[384,512]{1,0:T(8,128)S(1)}, u32[]{:S(2)}, u32[]{:S(2)}) collective-permute-start(f32[384,512]{1,0:T(8,128)S(1)} %shard_map.19), channel_id=1, source_target_pairs={{0,32},{32,0},{1,33},{33,1},{2,34},{34,2},{3,35},{35,3},{4,36},{36... | collective-permute-start | bytes 2359304 | tf_op jit(solution)/shard_map/ppermute | solution.py:237
  71.1 8.1 %collective-permute-start.2 = (f32[512,512]{1,0:T(8,128)S(1)}, f32[512,512]{1,0:T(8,128)S(1)}, u32[]{:S(2)}, u32[]{:S(2)}) collective-permute-start(f32[512,512]{1,0:T(8,128)S(1)} %get-tuple-element.8.own_ref), channel_id=1, source_target_pairs={{0,32},{32,0},{1,33},{33,1},{2,34},{34,2},{3,35},{35,3},{4,36},{36... | collective-permute-start | bytes 3145736 | tf_op jit(solution)/shard_map/ppermute | solution.py:237
  78.9 2.0 %collective-permute-start.1 = (bf16[512,512]{1,0:T(8,128)(2,1)S(1)}, bf16[512,512]{1,0:T(8,128)(2,1)S(1)}, u32[]{:S(2)}, u32[]{:S(2)}) collective-permute-start(bf16[512,512]{1,0:T(8,128)(2,1)S(1)} %shard_map.20.own_ref), channel_id=1, source_target_pairs={{0,32},{32,0},{1,33},{33,1},{2,34},{34,2},{3,35},{35,3},{4,36},{36... | collective-permute-start | bytes 1572872 | tf_op jit(solution)/shard_map/ppermute | solution.py:237

commit v11 on v8

--- a/solution.py
+++ b/solution.py
@@ -129,7 +129,7 @@
     )(blocks)
 
 
-def root_kernel(own_ref, other_ref, out_ref):
+def root_kernel(own_ref, other_ref, out_ref, packed_ref):
     row = lax.broadcasted_iota(jnp.int32, (QUARTER, QUARTER), 0)
     col = lax.broadcasted_iota(jnp.int32, (QUARTER, QUARTER), 1)
     diagonal = row == col
@@ -163,12 +163,15 @@
     for tile in tiles:
         x = scale * (jnp.where(diagonal, 1.0, 0.0) - y[tile, tile])
         out_ref[tile, tile] = x.astype(jnp.bfloat16)
+    store_gram(out_ref[:HALF], out_ref[HALF:, HALF:], packed_ref)
 
 
 def inverse_root(own, other):
     return pl.pallas_call(
         root_kernel,
-        out_shape=jax.ShapeDtypeStruct((BLOCK, BLOCK), jnp.bfloat16),
+        out_shape=[
+            jax.ShapeDtypeStruct((n, BLOCK), jnp.bfloat16) for n in (BLOCK, HALF + QUARTER)
+        ],
         compiler_params=pltpu.CompilerParams(vmem_limit_bytes=48 * 1024 * 1024),
         cost_estimate=pl.CostEstimate(
             flops=20 * 2 * BLOCK**3, bytes_accessed=10 * BLOCK * BLOCK, transcendentals=0
@@ -194,18 +197,22 @@
 def update_kernel(own_ref, other_ref, mean_ref, out_ref):
     side = lax.axis_index("core")
 
-    def piece(left_ref, right_ref, start):
-        right = right_ref[:, start : start + HALF]
+    packed = other_ref[...]
+    low = jnp.concatenate([packed[HALF:, :HALF], packed[HALF:, HALF:]], axis=0)
+    low = jnp.concatenate([packed[:HALF, HALF:].T, low], axis=1)
+    other = jnp.concatenate([packed[:HALF], low], axis=0)
+
+    def piece(left, right):
         inner = dot_nn(mean_ref[...], right).astype(jnp.bfloat16)
-        out_ref[...] = dot_nn(left_ref[...], inner).astype(jnp.bfloat16)
+        out_ref[...] = dot_nn(left, inner).astype(jnp.bfloat16)
 
     @pl.when(side == 0)
     def _():
-        piece(own_ref, other_ref, 0)
+        piece(own_ref[...], other[:, :HALF])
 
     @pl.when(side == 1)
     def _():
-        piece(other_ref, own_ref, HALF)
+        piece(other, own_ref[:, HALF:])
 
 
 def update_piece(own, other, mean):
@@ -228,8 +235,8 @@
     stat_other = swap_cores(other)
     keep, mean_own = gram(keep_kernel, (HALF + QUARTER, BLOCK), blocks)
     mean_other = swap_cores(mean_own)
-    own_root = inverse_root(keep, stat_other)
-    other_root = swap_cores(own_root)
+    own_root, packed_root = inverse_root(keep, stat_other)
+    other_root = swap_cores(packed_root)
     piece = update_piece(own_root, other_root, mean_block(mean_own, mean_other))
     rows = lax.all_to_all(
         piece.reshape(STRIPS, 16, HALF), ("y", "z"), split_axis=0, concat_axis=0, tiled=True

time: 100 us -> 100 us (level)
  no operation moved by 1% of the time
where the time goes in v11:
time: 100 us; the launch traced here: 99.9 us
  blocking collectives  84.7 us (85%)
  Pallas kernels  11.6 us (12%)
  waiting for transfers between devices  1.92 us (2%)
    all_to_all x1, blocking collectives, per_device(): lax.all_to_all(send, ('y', 'z', 'x'), split_axis=0, concat_axis=0, tiled=...  67.1 us
    all_to_all x1, blocking collectives, per_device(): lax.all_to_all(piece.reshape(STRIPS, 16, HALF), ('y', 'z'), split_axis=0,...  17.6 us
    pallas_call x1, Pallas kernels, inverse_root(): pl.pallas_call(root_kernel, out_shape=[jax.ShapeDtypeStruct((n, BLOCK), j...  6.88 us
    pallas_call x2, Pallas kernels, gram(): pl.pallas_call(kernel, out_shape=[jax.ShapeDtypeStruct((n, BLOCK), jnp.fl...  2.28 us
  transfers between devices with their start and end apart: 3, of which 2 were waited for; matrix products, arithmetic and copies ran while one was open for 0% of the time, Pallas kernels for 8%

profile of v11, /device:TPU:32, one launch (start us, length us, event | category | flops | bytes accessed | tf_op | source)
XLA Modules:
  0.0 99.9 jit_solution(9601219358301592247)
XLA Ops:
  0.0 1.6 %shard_map.17 = bf16[128,16,512]{2,1,0:T(8,128)(2,1)S(1)} custom-call(bf16[16,65536]{1,0:T(8,128)(2,1)} %bitcast.9), custom_call_target="tpu_custom_call" | custom-call | tf_op jit(solution)/shard_map/pallas_call | solution.py:57
  1.6 67.1 %all_to_all.10 = bf16[128,16,512]{2,1,0:T(8,128)(2,1)S(1)} all-to-all(bf16[128,16,512]{2,1,0:T(8,128)(2,1)S(1)} %shard_map.17), channel_id=1, replica_groups=mesh['x'=4,'core'=2,'y'=4,'z'=8] {'y','z','x'}, dimensions={0} | all-to-all | bytes 4194304 | tf_op jit(solution)/shard_map/all_to_all | solution.py:232
  68.7 1.0 %shard_map.19 = f32[384,512]{1,0:T(8,128)S(1)} custom-call(bf16[32,4,16,512]{3,2,1,0:T(8,128)(2,1)S(1)} %bitcast.6), custom_call_target="tpu_custom_call" | custom-call | flops 1073741824 | bytes 4194304 | tf_op jit(solution)/shard_map/pallas_call | solution.py:122
  69.7 0.1 collective-permute-start
  69.8 1.3 %shard_map.18 = (f32[384,512]{1,0:T(8,128)S(1)}, f32[512,512]{1,0:T(8,128)S(1)}) custom-call(bf16[32,4,16,512]{3,2,1,0:T(8,128)(2,1)S(1)} %bitcast.7), custom_call_target="tpu_custom_call" | custom-call | flops 1073741824 | bytes 4194304 | tf_op jit(solution)/shard_map/pallas_call | solution.py:122
  71.1 0.6 collective-permute-start.2
  71.7 0.4 collective-permute-done.other_ref
  72.1 6.9 %shard_map.20 = (bf16[512,512]{1,0:T(8,128)(2,1)S(1)}, bf16[384,512]{1,0:T(8,128)(2,1)S(1)}) custom-call(f32[384,512]{1,0:T(8,128)S(1)} %get-tuple-element.9.own_ref, f32[384,512]{1,0:T(8,128)S(1)} %collective-permute-done.other_ref), custom_call_target="tpu_custom_call" | custom-call | flops 5368709120 | bytes 2621440 | tf_op jit(solution)/shard_map/pallas_call | solution.py:170
  79.0 0.2 collective-permute-start.1
  79.2 0.0 collective-permute-done.2.other_ref
  79.2 0.1 shard_map.21.mean_ref
  79.3 1.5 %collective-permute-done.1.other_ref = bf16[384,512]{1,0:T(8,128)(2,1)S(1)} collective-permute-done((bf16[384,512]{1,0:T(8,128)(2,1)S(1)}, bf16[384,512]{1,0:T(8,128)(2,1)S(1)}, u32[]{:S(2)}, u32[]{:S(2)}) %collective-permute-start.1) | collective-permute-done | bytes 393248 | tf_op jit(solution)/shard_map/ppermute | solution.py:227
  80.8 0.8 shard_map.22
  81.6 17.6 %all_to_all.11 = bf16[32,16,256]{2,1,0:T(8,128)(2,1)S(1)} all-to-all(bf16[32,16,256]{2,1,0:T(8,128)(2,1)S(1)} %bitcast.8), channel_id=1, replica_groups=mesh['x'=4,'core'=2,'y'=4,'z'=8] {'y','z'}, dimensions={0} | all-to-all | bytes 524288 | tf_op jit(solution)/shard_map/all_to_all | solution.py:241
  99.2 0.8 copy.3
Async XLA Ops:
  69.7 2.4 %collective-permute-start = (f32[384,512]{1,0:T(8,128)S(1)}, f32[384,512]{1,0:T(8,128)S(1)}, u32[]{:S(2)}, u32[]{:S(2)}) collective-permute-start(f32[384,512]{1,0:T(8,128)S(1)} %shard_map.19), channel_id=1, source_target_pairs={{0,32},{32,0},{1,33},{33,1},{2,34},{34,2},{3,35},{35,3},{4,36},{36... | collective-permute-start | bytes 2359304 | tf_op jit(solution)/shard_map/ppermute | solution.py:227
  71.1 8.1 %collective-permute-start.2 = (f32[512,512]{1,0:T(8,128)S(1)}, f32[512,512]{1,0:T(8,128)S(1)}, u32[]{:S(2)}, u32[]{:S(2)}) collective-permute-start(f32[512,512]{1,0:T(8,128)S(1)} %get-tuple-element.12.own_ref), channel_id=1, source_target_pairs={{0,32},{32,0},{1,33},{33,1},{2,34},{34,2},{3,35},{35,3},{4,36},{36... | collective-permute-start | bytes 3145736 | tf_op jit(solution)/shard_map/ppermute | solution.py:227
  79.0 1.8 %collective-permute-start.1 = (bf16[384,512]{1,0:T(8,128)(2,1)S(1)}, bf16[384,512]{1,0:T(8,128)(2,1)S(1)}, u32[]{:S(2)}, u32[]{:S(2)}) collective-permute-start(bf16[384,512]{1,0:T(8,128)(2,1)S(1)} %get-tuple-element.11), channel_id=1, source_target_pairs={{0,32},{32,0},{1,33},{33,1},{2,34},{34,2},{3,35},{35,3},{4,36},{36... | collective-permute-start | bytes 1179656 | tf_op jit(solution)/shard_map/ppermute | solution.py:227
